TPU v7x, 128 devices: a whole 4x4x4 slice. The times are simulated.
128 devices in a mesh: slab: 32 (over y, z, core), cross: 4 (over x).
Axes of the slice: x: 4, y: 4, z: 4, core: 2. Of those that a mesh axis runs over, the one named last changes fastest.
Arguments:
- pressure_drive: float32 [3, 256, 256, 512], P(None, 'slab', 'cross'), may hold values from -23 to 23
- throat_radius: float32 [3, 256, 256, 512], P(None, 'slab', 'cross'), may hold values from 0.5 to 1.5
- wet_flag: int32 [3, 256, 256, 512], P(None, 'slab', 'cross'), may hold values 0 or 1
- cap_pressure: float32 [256, 256, 512], P('slab', 'cross'), may hold values from 1 to 3
- storage: float32 [256, 256, 512], P('slab', 'cross'), may hold values from 0.05 to 0.5
Outputs:
- solution: float32 [3, 256, 256, 512], P(None, 'slab', 'cross')
- residual: float32 [3, 256, 256, 512], P(None, 'slab', 'cross')
All inputs are finite; a program needn't handle non-finite values. No bound on the sum of `wet_flag` on one device may be relied on, other than what follows from the above.
Results may differ from a plain program's by a relative error of at most 0.0003.
Values sent between devices are 32-bit elements; how exact they have to be, the bound alone decides.
A program may use at most 128 MiB of HBM per device.

v0:
```python
import jax
import jax.numpy as jnp
from jax import lax
from jax.sharding import PartitionSpec as P

ITERS = 3


def shifted(value, axis, steps):
    count = lax.axis_size(axis)
    leading, last = (max(0, -steps), min(count, count - steps))
    return lax.ppermute(value, axis, [(source, source + steps) for source in range(leading, last)])


def with_halo(cells, sides, width):
    for axis, dim in sides:
        count = lax.axis_size(axis)
        ends = count - 1
        head = lax.slice_in_dim(cells, 0, width, axis=dim)
        tail = lax.slice_in_dim(cells, cells.shape[dim] - width, cells.shape[dim], axis=dim)
        cells = jnp.concatenate(
            [
                lax.ppermute(tail, axis, [(i, (i + 1) % count) for i in range(ends)]),
                cells,
                lax.ppermute(head, axis, [((i + 1) % count, i) for i in range(ends)]),
            ],
            axis=dim,
        )
    return cells


def totals(values):
    return jnp.sum(values, axis=(1, 2, 3))


def widen(scalars):
    return scalars[:, None, None, None]


def squares(residual):
    return lax.psum(totals(residual * residual), ("slab", "cross"))


def depth_terms(vector, along_depth, lower_depth):
    upper_values = jnp.pad(vector[..., 1:], ((0, 0), (0, 0), (0, 0), (0, 1)))
    lower_values = jnp.pad(vector[..., :-1], ((0, 0), (0, 0), (0, 0), (1, 0)))
    return along_depth * (vector - upper_values) + lower_depth * (vector - lower_values)


def per_device(pressure_drive, throat_radius, wet_flag, cap_pressure, storage):
    squared = throat_radius * throat_radius
    film_term = 0.4 * squared / (cap_pressure * cap_pressure)[None]
    conduct = jnp.where(wet_flag == 1, squared * squared, film_term)
    extent = conduct.shape[1:]
    layer_slab = lax.broadcasted_iota(jnp.int32, extent, 0)
    layer_cross = lax.broadcasted_iota(jnp.int32, extent, 1)
    layer_depth = lax.broadcasted_iota(jnp.int32, extent, 2)
    edge_slab = (layer_slab == extent[0] - 1) & (
        lax.axis_index("slab") == lax.axis_size("slab") - 1
    )
    edge_cross = (layer_cross == extent[1] - 1) & (
        lax.axis_index("cross") == lax.axis_size("cross") - 1
    )
    along_slab = jnp.where(edge_slab, 0.0, conduct[0])
    along_cross = jnp.where(edge_cross, 0.0, conduct[1])
    along_depth = jnp.where(layer_depth == extent[2] - 1, 0.0, conduct[2])
    lower_depth = jnp.pad(along_depth[:, :, :-1], ((0, 0), (0, 0), (1, 0)))
    rim_slab = shifted(along_slab[-1:], "slab", 1)
    rim_cross = shifted(along_cross[:, -1:], "cross", 1)
    lower_slab = jnp.concatenate([rim_slab, along_slab[:-1]], 0)
    lower_cross = jnp.concatenate([rim_cross, along_cross[:, :-1]], 1)
    solution = jnp.zeros_like(pressure_drive)
    residual = pressure_drive
    direction = pressure_drive
    norm_now = squares(residual)
    for iteration in range(ITERS):
        padded = with_halo(direction, (("slab", 1), ("cross", 2)), 1)
        result = storage * direction
        result = result + along_slab * (direction - padded[:, 2:, 1:-1])
        result = result + lower_slab * (direction - padded[:, :-2, 1:-1])
        result = result + along_cross * (direction - padded[:, 1:-1, 2:])
        result = result + lower_cross * (direction - padded[:, 1:-1, :-2])
        applied = result + depth_terms(direction, along_depth, lower_depth)
        step_size = norm_now / lax.psum(totals(direction * applied), ("slab", "cross"))
        solution = solution + widen(step_size) * direction
        residual = residual - widen(step_size) * applied
        if iteration + 1 < ITERS:
            norm_next = squares(residual)
            direction = residual + widen(norm_next / norm_now) * direction
            norm_now = norm_next
    return (solution, residual)


def solution(mesh):
    in_specs = (
        P(None, "slab", "cross", None),
        P(None, "slab", "cross", None),
        P(None, "slab", "cross", None),
        P("slab", "cross", None),
        P("slab", "cross", None),
    )
    out_specs = (P(None, "slab", "cross", None), P(None, "slab", "cross", None))
    return jax.shard_map(
        per_device, mesh=mesh, in_specs=in_specs, out_specs=out_specs, check_vma=False
    )
```

profile of v0, /device:TPU:1, one launch (start us, length us, event | category | flops | bytes accessed | tf_op | source)
XLA Modules:
  0.0 452.4 jit_solution(15411838793907103219)
XLA Ops:
  0.6 2.1 fusion.47
  2.7 3.3 collective-permute-start
  6.0 3.5 collective-permute-start.2
  12.1 2.8 divide_select_fusion
  15.3 3.2 collective-permute-start.4
  18.6 2.7 collective-permute-start.1
  26.9 4.0 collective-permute-start.5
  32.2 8.0 %multiply_reduce_fusion.4 = (f32[3]{0:T(128)S(1)}, f32[3]{0:T(128)S(1)}, f32[3,8,64,512]{3,2,1,0:T(8,128)}) fusion(f32[3,8,64,512]{3,2,1,0:T(8,128)S(1)} %copy-done, f32[3,8,64,511]{3,2,1,0:T(8,128)S(1)} %get-tuple-element.36, f32[8,64,512]{2,1,0:T(8,128)S(1)} %pad.25, f32[3,8,64,511]{3,2,1,0:T(8,128)S(1)} %get-tuple-element.35, ...), kind=kLoop, calls=%fused_computation.69 | loop fusion | flops 21233656 | bytes 24752152 | tf_op jit(solution)/shard_map/reduce_sum | solution.py:33
  40.3 68.6 %all-reduce.7 = (f32[3]{0:T(128)S(1)}, f32[3]{0:T(128)S(1)}) all-reduce(f32[3]{0:T(128)S(1)} %get-tuple-element.3, f32[3]{0:T(128)S(1)} %get-tuple-element.2), channel_id=1, replica_groups=mesh['slab'=32,'cross'=4] {'slab','cross'}, use_global_device_ids=true, to_apply=%region_1.2 | all-reduce | flops 6 | bytes 48 | tf_op jit(solution)/shard_map/psum | solution.py:41
  108.9 2.6 multiply_reduce_fusion.3
  111.5 63.8 %psum.44 = f32[3]{0:T(128)S(1)} all-reduce(f32[3]{0:T(128)S(1)} %multiply_reduce_fusion.3), channel_id=1, replica_groups=mesh['slab'=32,'cross'=4] {'slab','cross'}, use_global_device_ids=true, to_apply=%region_5.6 | all-reduce | flops 3 | bytes 24 | tf_op jit(solution)/shard_map/psum | solution.py:41
  175.2 2.7 multiply_add_fusion.2
  178.1 1.9 collective-permute-start.7
  180.0 2.4 collective-permute-start.6
  182.4 2.3 collective-permute-done.7
  184.7 4.7 %collective-permute-done.6 = f32[3,1,64,512]{3,2,1,0:T(8,128)S(1)} collective-permute-done((f32[3,1,64,512]{3,2,1,0:T(8,128)S(1)}, f32[3,1,64,512]{3,2,1,0:T(8,128)S(1)}, u32[]{:S(2)}, u32[]{:S(2)}) %collective-permute-start.6) | collective-permute-done | bytes 393248 | tf_op jit(solution)/shard_map/ppermute | solution.py:25
  190.9 4.4 collective-permute-start.9
  195.3 2.8 fusion.46
  198.2 8.7 %multiply_reduce_fusion.2 = (f32[3]{0:T(128)}, f32[3,8,64,512]{3,2,1,0:T(8,128)}) fusion(f32[3,8,64,512]{3,2,1,0:T(8,128)S(1)} %multiply_add_fusion.2, f32[3,8,64,511]{3,2,1,0:T(8,128)} %get-tuple-element.26, f32[8,64,512]{2,1,0:T(8,128)S(1)} %copy-done.4, f32[3,8,64,511]{3,2,1,0:T(8,128)S(1)} %get-tuple-element.25, f32[8,64,512]{2,1,0:T(8,128)S(1)} %copy-done.16, ...), kind=kLoop, calls=%fused_computation.65 | loop fusion | flops 22806524 | bytes 20819980 | tf_op jit(solution)/shard_map/reduce_sum | solution.py:33
  206.9 66.3 %psum.45 = f32[3]{0:T(128)S(1)} all-reduce(f32[3]{0:T(128)} %get-tuple-element.10), channel_id=1, replica_groups=mesh['slab'=32,'cross'=4] {'slab','cross'}, use_global_device_ids=true, to_apply=%region_7.8 | all-reduce | flops 3 | bytes 24 | tf_op jit(solution)/shard_map/psum | solution.py:84
  273.9 5.4 %multiply_reduce_fusion.1 = (f32[3]{0:T(128)S(1)}, f32[3,8,64,512]{3,2,1,0:T(8,128)}) fusion(f32[3,8,64,512]{3,2,1,0:T(8,128)} %get-tuple-element.11, f32[3]{0:T(128)S(1)} %div.27, f32[3,8,64,512]{3,2,1,0:T(8,128)S(1)} %copy-done, f32[3,8,64,512]{3,2,1,0:T(8,128)} %get-tuple-element.12, f32[3]{0:T(128)S(1)} %div.25), kind=kLoop, calls=%fused_computation.63 | loop fusion | flops 4718589 | bytes 12582948 | tf_op jit(solution)/shard_map/reduce_sum | solution.py:33
  279.3 63.4 %psum.46 = f32[3]{0:T(128)S(1)} all-reduce(f32[3]{0:T(128)S(1)} %get-tuple-element.8), channel_id=1, replica_groups=mesh['slab'=32,'cross'=4] {'slab','cross'}, use_global_device_ids=true, to_apply=%region_9.10 | all-reduce | flops 3 | bytes 24 | tf_op jit(solution)/shard_map/psum | solution.py:41
  342.7 3.7 multiply_add_fusion.1
  346.5 2.1 collective-permute-start.11
  348.6 2.2 collective-permute-start.10
  350.8 2.5 collective-permute-done.11
  353.3 4.7 %collective-permute-done.10 = f32[3,1,64,512]{3,2,1,0:T(8,128)S(1)} collective-permute-done((f32[3,1,64,512]{3,2,1,0:T(8,128)S(1)}, f32[3,1,64,512]{3,2,1,0:T(8,128)S(1)}, u32[]{:S(2)}, u32[]{:S(2)}) %collective-permute-start.10) | collective-permute-done | bytes 393248 | tf_op jit(solution)/shard_map/ppermute | solution.py:25
  359.5 4.3 collective-permute-start.13
  363.8 2.8 fusion.44
  366.7 8.7 %multiply_reduce_fusion = (f32[3]{0:T(128)}, f32[3,8,64,512]{3,2,1,0:T(8,128)}) fusion(f32[3,8,64,512]{3,2,1,0:T(8,128)S(1)} %multiply_add_fusion.1, f32[3,8,64,511]{3,2,1,0:T(8,128)} %get-tuple-element.22, f32[8,64,512]{2,1,0:T(8,128)S(1)} %copy-done.5, f32[3,8,64,511]{3,2,1,0:T(8,128)S(1)} %get-tuple-element.21, f32[8,64,512]{2,1,0:T(8,128)S(1)} %copy-done.17, ...), kind=kLoop, calls=%fused_computation.61 | loop fusion | flops 22806524 | bytes 20819980 | tf_op jit(solution)/shard_map/reduce_sum | solution.py:33
  375.4 66.4 %psum.47 = f32[3]{0:T(128)S(1)} all-reduce(f32[3]{0:T(128)} %get-tuple-element.6), channel_id=1, replica_groups=mesh['slab'=32,'cross'=4] {'slab','cross'}, use_global_device_ids=true, to_apply=%region_11.12 | all-reduce | flops 3 | bytes 24 | tf_op jit(solution)/shard_map/psum | solution.py:84
  442.4 10.0 %multiply_subtract_fusion = (f32[3,8,64,512]{3,2,1,0:T(8,128)}, f32[3,8,64,512]{3,2,1,0:T(8,128)}) fusion(f32[3,8,64,512]{3,2,1,0:T(8,128)} %get-tuple-element.9, f32[3,8,64,512]{3,2,1,0:T(8,128)} %get-tuple-element.7, f32[3]{0:T(128)S(1)} %div.29, f32[3,8,64,512]{3,2,1,0:T(8,128)} %copy-done.2, f32[3,8,64,512]{3,2,1,0:T(8,128)} %copy-done.1, ...), kind=kLoop, calls=%fused_computation.59 | loop fusion | flops 5505024 | bytes 22020132 | tf_op jit(solution)/shard_map/sub | solution.py:86
  (100 shorter events, 13.9 us)
Async XLA Ops:
  2.7 22.7 %collective-permute-start = (f32[3,1,64,512]{3,2,1,0:T(8,128)}, f32[3,1,64,512]{3,2,1,0:T(8,128)S(1)}, u32[]{:S(2)}, u32[]{:S(2)}) collective-permute-start(f32[3,1,64,512]{3,2,1,0:T(8,128)} %get-tuple-element.33), channel_id=1, source_target_pairs={{4,0},{8,4},{12,8},{16,12},{20,16},{24,20},{28,24},{32,28},{36,32}... | collective-permute-start | bytes 1179656 | tf_op jit(solution)/shard_map/ppermute | solution.py:25
  6.0 17.8 %collective-permute-start.2 = (f32[3,1,64,512]{3,2,1,0:T(8,128)}, f32[3,1,64,512]{3,2,1,0:T(8,128)}, u32[]{:S(2)}, u32[]{:S(2)}) collective-permute-start(f32[3,1,64,512]{3,2,1,0:T(8,128)} %get-tuple-element.34), channel_id=1, source_target_pairs={{0,4},{4,8},{8,12},{12,16},{16,20},{20,24},{24,28},{28,32},{32,36}... | collective-permute-start | bytes 1179656 | tf_op jit(solution)/shard_map/ppermute | solution.py:23
  15.3 8.3 %collective-permute-start.4 = (f32[8,1,512]{2,1,0:T(1,128)S(1)}, f32[8,1,512]{2,1,0:T(1,128)S(1)}, u32[]{:S(2)}, u32[]{:S(2)}) collective-permute-start(f32[8,1,512]{2,1,0:T(1,128)S(1)} %slice.169), channel_id=1, source_target_pairs={{0,1},{1,2},{2,3},{4,5},{5,6},{6,7},{8,9},{9,10},{10,11},{12,13},{... | collective-permute-start | bytes 49160 | tf_op jit(solution)/shard_map/ppermute | solution.py:12
  18.6 12.4 %collective-permute-start.1 = (f32[1,64,512]{2,1,0:T(8,128)S(1)}, f32[1,64,512]{2,1,0:T(8,128)S(1)}, u32[]{:S(2)}, u32[]{:S(2)}) collective-permute-start(f32[1,64,512]{2,1,0:T(8,128)S(1)} %slice.165), channel_id=1, source_target_pairs={{0,4},{4,8},{8,12},{12,16},{16,20},{20,24},{24,28},{28,32},{32,36}... | collective-permute-start | bytes 393224 | tf_op jit(solution)/shard_map/ppermute | solution.py:12
  23.0 9.2 %copy-start.12 = (f32[8,64,512]{2,1,0:T(8,128)}, f32[8,64,512]{2,1,0:T(8,128)S(1)}, u32[]{:S(2)}) copy-start(f32[8,64,512]{2,1,0:T(8,128)S(1)} %get-tuple-element.27) | copy-start | bytes 3145732
  23.0 9.2 %copy-start.15 = (f32[8,64,512]{2,1,0:T(8,128)}, f32[8,64,512]{2,1,0:T(8,128)S(1)}, u32[]{:S(2)}) copy-start(f32[8,64,512]{2,1,0:T(8,128)S(1)} %get-tuple-element.29) | copy-start | bytes 3145732
  23.0 9.2 %copy-start.18 = (f32[8,64,512]{2,1,0:T(8,128)}, f32[8,64,512]{2,1,0:T(8,128)S(1)}, u32[]{:S(2)}) copy-start(f32[8,64,512]{2,1,0:T(8,128)S(1)} %get-tuple-element.30) | copy-start | bytes 3145732
  23.6 8.6 %copy-start.3 = (f32[8,64,512]{2,1,0:T(8,128)}, f32[8,64,512]{2,1,0:T(8,128)S(1)}, u32[]{:S(2)}) copy-start(f32[8,64,512]{2,1,0:T(8,128)S(1)} %pad.25) | copy-start | bytes 3145732
  23.8 8.4 %copy-start.6 = (f32[8,64,512]{2,1,0:T(8,128)}, f32[8,64,512]{2,1,0:T(8,128)S(1)}, u32[]{:S(2)}) copy-start(f32[8,64,512]{2,1,0:T(8,128)S(1)} %pad_maximum_fusion.21) | copy-start | bytes 3145732
  25.6 5.7 %collective-permute-start.3 = (f32[3,10,1,512]{3,2,1,0:T(1,128)S(1)}, f32[3,10,1,512]{3,2,1,0:T(1,128)S(1)}, u32[]{:S(2)}, u32[]{:S(2)}) collective-permute-start(f32[3,10,1,512]{3,2,1,0:T(1,128)S(1)} %get-tuple-element.17), channel_id=1, source_target_pairs={{1,0},{2,1},{3,2},{5,4},{6,5},{7,6},{9,8},{10,9},{11,10},{13,12},{... | collective-permute-start | bytes 184328 | tf_op jit(solution)/shard_map/ppermute | solution.py:25
  26.9 5.3 %collective-permute-start.5 = (f32[3,10,1,512]{3,2,1,0:T(1,128)S(1)}, f32[3,10,1,512]{3,2,1,0:T(1,128)S(1)}, u32[]{:S(2)}, u32[]{:S(2)}) collective-permute-start(f32[3,10,1,512]{3,2,1,0:T(1,128)S(1)} %get-tuple-element.18), channel_id=1, source_target_pairs={{0,1},{1,2},{2,3},{4,5},{5,6},{6,7},{8,9},{9,10},{10,11},{12,13},{... | collective-permute-start | bytes 184328 | tf_op jit(solution)/shard_map/ppermute | solution.py:23
  31.0 9.3 %copy-start.9 = (f32[8,64,512]{2,1,0:T(8,128)}, f32[8,64,512]{2,1,0:T(8,128)S(1)}, u32[]{:S(2)}) copy-start(f32[8,64,512]{2,1,0:T(8,128)S(1)} %pad_maximum_fusion.20) | copy-start | bytes 3145732
  178.0 20.2 %copy-start.1 = (f32[3,8,64,512]{3,2,1,0:T(8,128)}, f32[3,8,64,512]{3,2,1,0:T(8,128)S(1)}, u32[]{:S(2)}) copy-start(f32[3,8,64,512]{3,2,1,0:T(8,128)S(1)} %multiply_add_fusion.2) | copy-start | bytes 9437188
  178.1 6.6 %collective-permute-start.7 = (f32[3,1,64,512]{3,2,1,0:T(8,128)S(1)}, f32[3,1,64,512]{3,2,1,0:T(8,128)S(1)}, u32[]{:S(2)}, u32[]{:S(2)}) collective-permute-start(f32[3,1,64,512]{3,2,1,0:T(8,128)S(1)} %get-tuple-element.23), channel_id=1, source_target_pairs={{0,4},{4,8},{8,12},{12,16},{16,20},{20,24},{24,28},{28,32},{32,36}... | collective-permute-start | bytes 1179656 | tf_op jit(solution)/shard_map/ppermute | solution.py:23
  180.0 9.4 %collective-permute-start.6 = (f32[3,1,64,512]{3,2,1,0:T(8,128)S(1)}, f32[3,1,64,512]{3,2,1,0:T(8,128)S(1)}, u32[]{:S(2)}, u32[]{:S(2)}) collective-permute-start(f32[3,1,64,512]{3,2,1,0:T(8,128)S(1)} %get-tuple-element.24), channel_id=1, source_target_pairs={{4,0},{8,4},{12,8},{16,12},{20,16},{24,20},{28,24},{32,28},{36,32}... | collective-permute-start | bytes 1179656 | tf_op jit(solution)/shard_map/ppermute | solution.py:25
  189.5 8.7 %collective-permute-start.8 = (f32[3,10,1,512]{3,2,1,0:T(1,128)S(1)}, f32[3,10,1,512]{3,2,1,0:T(1,128)S(1)}, u32[]{:S(2)}, u32[]{:S(2)}) collective-permute-start(f32[3,10,1,512]{3,2,1,0:T(1,128)S(1)} %get-tuple-element.15), channel_id=1, source_target_pairs={{1,0},{2,1},{3,2},{5,4},{6,5},{7,6},{9,8},{10,9},{11,10},{13,12},{... | collective-permute-start | bytes 184328 | tf_op jit(solution)/shard_map/ppermute | solution.py:25
  190.8 7.4 %copy-start.4 = (f32[8,64,512]{2,1,0:T(8,128)S(1)}, f32[8,64,512]{2,1,0:T(8,128)}, u32[]{:S(2)}) copy-start(f32[8,64,512]{2,1,0:T(8,128)} %copy-done.3) | copy-start | bytes 3145732
  190.8 7.4 %copy-start.7 = (f32[8,64,512]{2,1,0:T(8,128)S(1)}, f32[8,64,512]{2,1,0:T(8,128)}, u32[]{:S(2)}) copy-start(f32[8,64,512]{2,1,0:T(8,128)} %copy-done.6) | copy-start | bytes 3145732
  190.8 7.4 %copy-start.10 = (f32[8,64,512]{2,1,0:T(8,128)S(1)}, f32[8,64,512]{2,1,0:T(8,128)}, u32[]{:S(2)}) copy-start(f32[8,64,512]{2,1,0:T(8,128)} %copy-done.9) | copy-start | bytes 3145732
  190.9 7.4 %copy-start.13 = (f32[8,64,512]{2,1,0:T(8,128)S(1)}, f32[8,64,512]{2,1,0:T(8,128)}, u32[]{:S(2)}) copy-start(f32[8,64,512]{2,1,0:T(8,128)} %copy-done.12) | copy-start | bytes 3145732
  190.9 7.4 %copy-start.16 = (f32[8,64,512]{2,1,0:T(8,128)S(1)}, f32[8,64,512]{2,1,0:T(8,128)}, u32[]{:S(2)}) copy-start(f32[8,64,512]{2,1,0:T(8,128)} %copy-done.15) | copy-start | bytes 3145732
  190.9 7.4 %copy-start.19 = (f32[8,64,512]{2,1,0:T(8,128)S(1)}, f32[8,64,512]{2,1,0:T(8,128)}, u32[]{:S(2)}) copy-start(f32[8,64,512]{2,1,0:T(8,128)} %copy-done.18) | copy-start | bytes 3145732
  190.9 7.3 %collective-permute-start.9 = (f32[3,10,1,512]{3,2,1,0:T(1,128)S(1)}, f32[3,10,1,512]{3,2,1,0:T(1,128)S(1)}, u32[]{:S(2)}, u32[]{:S(2)}) collective-permute-start(f32[3,10,1,512]{3,2,1,0:T(1,128)S(1)} %get-tuple-element.16), channel_id=1, source_target_pairs={{0,1},{1,2},{2,3},{4,5},{5,6},{6,7},{8,9},{9,10},{10,11},{12,13},{... | collective-permute-start | bytes 184328 | tf_op jit(solution)/shard_map/ppermute | solution.py:23
  273.9 68.8 %copy-start.28 = (f32[3]{0:T(128)S(1)}, f32[3]{0:T(128)}, u32[]{:S(2)}) copy-start(f32[3]{0:T(128)} %copy-done.27) | copy-start | bytes 40
  346.4 20.2 %copy-start.2 = (f32[3,8,64,512]{3,2,1,0:T(8,128)}, f32[3,8,64,512]{3,2,1,0:T(8,128)S(1)}, u32[]{:S(2)}) copy-start(f32[3,8,64,512]{3,2,1,0:T(8,128)S(1)} %multiply_add_fusion.1) | copy-start | bytes 9437188
  346.5 6.8 %collective-permute-start.11 = (f32[3,1,64,512]{3,2,1,0:T(8,128)S(1)}, f32[3,1,64,512]{3,2,1,0:T(8,128)S(1)}, u32[]{:S(2)}, u32[]{:S(2)}) collective-permute-start(f32[3,1,64,512]{3,2,1,0:T(8,128)S(1)} %get-tuple-element.19), channel_id=1, source_target_pairs={{0,4},{4,8},{8,12},{12,16},{16,20},{20,24},{24,28},{28,32},{32,36}... | collective-permute-start | bytes 1179656 | tf_op jit(solution)/shard_map/ppermute | solution.py:23
  348.6 9.4 %collective-permute-start.10 = (f32[3,1,64,512]{3,2,1,0:T(8,128)S(1)}, f32[3,1,64,512]{3,2,1,0:T(8,128)S(1)}, u32[]{:S(2)}, u32[]{:S(2)}) collective-permute-start(f32[3,1,64,512]{3,2,1,0:T(8,128)S(1)} %get-tuple-element.20), channel_id=1, source_target_pairs={{4,0},{8,4},{12,8},{16,12},{20,16},{24,20},{28,24},{32,28},{36,32}... | collective-permute-start | bytes 1179656 | tf_op jit(solution)/shard_map/ppermute | solution.py:25
  358.1 8.5 %collective-permute-start.12 = (f32[3,10,1,512]{3,2,1,0:T(1,128)S(1)}, f32[3,10,1,512]{3,2,1,0:T(1,128)S(1)}, u32[]{:S(2)}, u32[]{:S(2)}) collective-permute-start(f32[3,10,1,512]{3,2,1,0:T(1,128)S(1)} %get-tuple-element.13), channel_id=1, source_target_pairs={{1,0},{2,1},{3,2},{5,4},{6,5},{7,6},{9,8},{10,9},{11,10},{13,12},{... | collective-permute-start | bytes 184328 | tf_op jit(solution)/shard_map/ppermute | solution.py:25
  359.4 7.2 %copy-start.5 = (f32[8,64,512]{2,1,0:T(8,128)S(1)}, f32[8,64,512]{2,1,0:T(8,128)}, u32[]{:S(2)}) copy-start(f32[8,64,512]{2,1,0:T(8,128)} %copy-done.3) | copy-start | bytes 3145732
  359.4 7.2 %copy-start.8 = (f32[8,64,512]{2,1,0:T(8,128)S(1)}, f32[8,64,512]{2,1,0:T(8,128)}, u32[]{:S(2)}) copy-start(f32[8,64,512]{2,1,0:T(8,128)} %copy-done.6) | copy-start | bytes 3145732
  359.5 7.2 %copy-start.11 = (f32[8,64,512]{2,1,0:T(8,128)S(1)}, f32[8,64,512]{2,1,0:T(8,128)}, u32[]{:S(2)}) copy-start(f32[8,64,512]{2,1,0:T(8,128)} %copy-done.9) | copy-start | bytes 3145732
  359.5 7.1 %collective-permute-start.13 = (f32[3,10,1,512]{3,2,1,0:T(1,128)S(1)}, f32[3,10,1,512]{3,2,1,0:T(1,128)S(1)}, u32[]{:S(2)}, u32[]{:S(2)}) collective-permute-start(f32[3,10,1,512]{3,2,1,0:T(1,128)S(1)} %get-tuple-element.14), channel_id=1, source_target_pairs={{0,1},{1,2},{2,3},{4,5},{5,6},{6,7},{8,9},{9,10},{10,11},{12,13},{... | collective-permute-start | bytes 184328 | tf_op jit(solution)/shard_map/ppermute | solution.py:23
  (12 other events, 57.5 us)
where the time goes:
time: 454 us; the launch traced here: 452 us
  blocking collectives  329 us (72%)
  other arithmetic  57.2 us (13%)
  starting transfers between devices  38 us (8%)
  waiting for transfers between devices  15.3 us (3%)
  local copies, waits for them, and re-layouts  12 us (3%)
    psum x3, blocking collectives, squares(): return lax.psum(totals(residual * residual), ('slab', 'cross'))  196 us
    psum x2, blocking collectives, per_device(): lax.psum(totals(direction * applied), ('slab', 'cross'))  133 us
    reduce_sum x5, other arithmetic, totals(): return jnp.sum(values, axis=(1, 2, 3))  33.4 us
    ppermute x6, starting transfers between devices, with_halo(): lax.ppermute(tail, axis, [(i, (i + 1) % count) for i in range(ends)])  20.3 us
    ppermute x6, starting transfers between devices, with_halo(): lax.ppermute(head, axis, [((i + 1) % count, i) for i in range(ends)])  11.8 us
    sub x1, other arithmetic, per_device(): residual = residual - widen(step_size) * applied  10 us
    ppermute x6, waiting for transfers between devices, with_halo(): lax.ppermute(head, axis, [((i + 1) % count, i) for i in range(ends)])  9.7 us
  transfers between devices with their start and end apart: 14, of which 6 were waited for; matrix products, arithmetic and copies ran while one was open for 3% of the time, Pallas kernels for 0%

commit v1 on v0

--- a/solution.py
+++ b/solution.py
@@ -1,9 +1,21 @@
+import functools
+
 import jax
 import jax.numpy as jnp
 from jax import lax
+from jax.experimental import pallas as pl
+from jax.experimental.pallas import tpu as pltpu
 from jax.sharding import PartitionSpec as P
 
 ITERS = 3
+RHS = 3
+F32 = jnp.float32
+MESH = pl.DeviceIdType.MESH
+SLABS, CROSSES = 32, 4
+LA, LB, NC = 8, 64, 512
+TILES = LB // 8
+ERROR_GAIN_MAX = 2500.0
+CANCEL_MAX = 300.0
 
 
 def shifted(value, axis, steps):
@@ -47,7 +59,7 @@
     return along_depth * (vector - upper_values) + lower_depth * (vector - lower_values)
 
 
-def per_device(pressure_drive, throat_radius, wet_flag, cap_pressure, storage):
+def plain_iteration(pressure_drive, throat_radius, wet_flag, cap_pressure, storage):
     squared = throat_radius * throat_radius
     film_term = 0.4 * squared / (cap_pressure * cap_pressure)[None]
     conduct = jnp.where(wet_flag == 1, squared * squared, film_term)
@@ -91,6 +103,388 @@
     return (solution, residual)
 
 
+def scalars_of(m):
+    def parts(c0, c1, c2, first):
+        return (
+            c0 * c0 * m[first],
+            2.0 * c0 * c1 * m[first + 1],
+            c1 * c1 * m[first + 2],
+            2.0 * c0 * c2 * m[first + 2],
+            2.0 * c1 * c2 * m[first + 3],
+            c2 * c2 * m[first + 4],
+        )
+
+    def total(terms):
+        return (terms[0] + terms[1]) + (terms[2] + terms[3]) + (terms[4] + terms[5])
+
+    def bulk(terms):
+        return total([jnp.abs(term) for term in terms])
+
+    rr0 = m[0]
+    step0 = m[0] / m[1]
+    image0 = step0 * step0 * m[2]
+    rr1 = image0 - rr0
+    turn0 = rr1 / rr0
+    p0, p1 = 1.0 + turn0, -step0
+
+    def pair(first):
+        return p0 * p0 * m[first], 2.0 * p0 * p1 * m[first + 1], p1 * p1 * m[first + 2]
+
+    energy1 = pair(1)
+    curve1 = energy1[0] + energy1[1] + energy1[2]
+    step1 = rr1 / curve1
+    image1 = pair(2)
+    rr2 = step1 * step1 * (image1[0] + image1[1] + image1[2]) - rr1
+    turn1 = rr2 / rr1
+    r1, r2 = -step0 - step1 * p0, -step1 * p1
+    q0, q1, q2 = 1.0 + turn1 * p0, r1 + turn1 * p1, r2
+    energy2 = parts(q0, q1, q2, 1)
+    curve2 = total(energy2)
+    step2 = rr2 / curve2
+    x0 = step0 + step1 * p0 + step2 * q0
+    x1 = step1 * p1 + step2 * q1
+    x2 = step2 * q2
+    d1, d2, d3 = r1 - step2 * q0, r2 - step2 * q1, -step2 * q2
+
+    image2 = parts(q0, q1, q2, 2)
+    rr3 = step2 * step2 * total(image2) - rr2
+    gain1 = (image0 + rr0) / rr1
+    gain2 = (energy1[0] + jnp.abs(energy1[1]) + energy1[2]) / curve1
+    gain3 = (step1 * step1 * (image1[0] + jnp.abs(image1[1]) + image1[2]) + rr1) / rr2
+    gain4 = bulk(energy2) / curve2
+    gain5 = (step2 * step2 * bulk(image2) + rr2) / rr3
+    gain = (
+        (gain1 + gain2) * jnp.sqrt(rr0 / rr3)
+        + gain3 * jnp.sqrt(rr1 / rr3)
+        + gain4 * jnp.sqrt(rr2 / rr3)
+        + gain5
+    )
+    cancel = (
+        jnp.sqrt(m[0])
+        + jnp.abs(d1) * jnp.sqrt(m[2])
+        + jnp.abs(d2) * jnp.sqrt(m[4])
+        + jnp.abs(d3) * jnp.sqrt(m[6])
+    ) / jnp.sqrt(rr3)
+    sound = (
+        (rr1 > 0.0)
+        & (curve1 > 0.0)
+        & (rr2 > 0.0)
+        & (curve2 > 0.0)
+        & (rr3 > 0.0)
+        & (gain < ERROR_GAIN_MAX)
+        & (cancel < CANCEL_MAX)
+    )
+    return (x0, x1, x2, d1, d2, d3), sound
+
+
+def fold(value):
+    return (value[:, 0:128] + value[:, 128:256]) + (value[:, 256:384] + value[:, 384:512])
+
+
+def powers_kernel(
+    b_hbm, rad_hbm, wet_hbm, cap_hbm, sto_hbm,
+    v0, v1, v2, v3, coef_ref, sound_ref,
+    cond, wet, cap, sto, cs_low, cc_out, cc_low,
+    halo_low, halo_up, edge_low, edge_up, rim_low, rim_up,
+    flux, moments, sent1, sent2, got1, got2,
+    load_sem, halo_send, halo_recv, cond_send, cond_recv, sum_send, sum_recv,
+):
+    s, c = lax.axis_index("slab"), lax.axis_index("cross")
+    up, down = lax.rem(s + 1, SLABS), lax.rem(s + SLABS - 1, SLABS)
+    right, left = lax.rem(c + 1, CROSSES), lax.rem(c + CROSSES - 1, CROSSES)
+    row_y, in_row = s // 8, lax.rem(s, 8)
+    group1 = [(row_y * 8 + lax.rem(in_row + i, 8), c) for i in range(1, 8)]
+    group2 = [
+        (lax.rem(row_y + i, 4) * 8 + in_row, lax.rem(c + j, 4))
+        for i in range(4)
+        for j in range(4)
+        if i or j
+    ]
+    barrier = pltpu.get_barrier_semaphore()
+    greeted = [(up, c), (down, c), (s, right), (s, left)] + group1 + group2
+    for peer in greeted:
+        pl.semaphore_signal(barrier, inc=1, device_id=peer, device_id_type=MESH)
+
+    loads = [
+        pltpu.make_async_copy(rad_hbm, cond, load_sem.at[0]),
+        pltpu.make_async_copy(wet_hbm, wet, load_sem.at[1]),
+        pltpu.make_async_copy(cap_hbm, cap, load_sem.at[2]),
+        pltpu.make_async_copy(b_hbm, v0, load_sem.at[3]),
+        pltpu.make_async_copy(sto_hbm, sto, load_sem.at[4]),
+    ]
+    for load in loads:
+        load.start()
+    for load in loads[:3]:
+        load.wait()
+
+    row = lax.broadcasted_iota(jnp.int32, (8, NC), 0)
+    lane = lax.broadcasted_iota(jnp.int32, (8, NC), 1)
+    first_row, last_row, last_lane = row == 0, row == 7, lane == NC - 1
+
+    def conduct(a, carry):
+        ends_slab = (s == SLABS - 1) & (a == LA - 1)
+        for j in range(TILES):
+            at = pl.ds(8 * j, 8)
+            pressure = cap[a, at, :]
+            film = 0.4 / (pressure * pressure)
+            for k in range(3):
+                radius = cond[k, a, at, :]
+                squared = radius * radius
+                value = squared * jnp.where(wet[k, a, at, :] == 1, squared, film)
+                if k == 0:
+                    value = jnp.where(ends_slab, 0.0, value)
+                if k == 1 and j == TILES - 1:
+                    value = jnp.where(last_row & (c == CROSSES - 1), 0.0, value)
+                    cc_out[a] = value[7:8, :]
+                if k == 2:
+                    value = jnp.where(last_lane, 0.0, value)
+                cond[k, a, at, :] = value
+        return carry
+
+    lax.fori_loop(0, LA, conduct, 0)
+
+    loads[3].wait()
+    for q in range(RHS):
+        for a in range(LA):
+            edge_low[0, q, a] = v0[q, a, 0:1, :]
+            edge_up[0, q, a] = v0[q, a, LB - 1 : LB, :]
+    loads[4].wait()
+    moments[...] = jnp.zeros_like(moments)
+    pl.semaphore_wait(barrier, len(greeted))
+
+    vectors = (v0, v1, v2, v3)
+
+    def halo_copies(k, q):
+        v = vectors[k]
+        return (
+            pltpu.make_async_remote_copy(
+                src_ref=v.at[q, 0], dst_ref=halo_up.at[k, q], send_sem=halo_send.at[k, q, 0],
+                recv_sem=halo_recv.at[k, q, 0], device_id=(down, c), device_id_type=MESH),
+            pltpu.make_async_remote_copy(
+                src_ref=v.at[q, LA - 1], dst_ref=halo_low.at[k, q], send_sem=halo_send.at[k, q, 1],
+                recv_sem=halo_recv.at[k, q, 1], device_id=(up, c), device_id_type=MESH),
+            pltpu.make_async_remote_copy(
+                src_ref=edge_low.at[k, q], dst_ref=rim_up.at[k, q], send_sem=halo_send.at[k, q, 2],
+                recv_sem=halo_recv.at[k, q, 2], device_id=(s, left), device_id_type=MESH),
+            pltpu.make_async_remote_copy(
+                src_ref=edge_up.at[k, q], dst_ref=rim_low.at[k, q], send_sem=halo_send.at[k, q, 3],
+                recv_sem=halo_recv.at[k, q, 3], device_id=(s, right), device_id_type=MESH),
+        )
+
+    cond_copies = (
+        pltpu.make_async_remote_copy(
+            src_ref=cond.at[0, LA - 1], dst_ref=cs_low, send_sem=cond_send.at[0],
+            recv_sem=cond_recv.at[0], device_id=(up, c), device_id_type=MESH),
+        pltpu.make_async_remote_copy(
+            src_ref=cc_out, dst_ref=cc_low, send_sem=cond_send.at[1],
+            recv_sem=cond_recv.at[1], device_id=(s, right), device_id_type=MESH),
+    )
+    for q in range(RHS):
+        for copy in halo_copies(0, q):
+            copy.start()
+        if q == 0:
+            for copy in cond_copies:
+                copy.start()
+    for copy in cond_copies:
+        copy.wait_recv()
+
+    def spread(line):
+        return jnp.broadcast_to(line, (8, NC))
+
+    for k in range(ITERS):
+        v, w = vectors[k], vectors[k + 1]
+
+        def layer(q, a, above, carry):
+            dots = carry
+            here = v[q, a, 0:8, :]
+            here_up = pltpu.roll(here, 7, 0)
+            passed = spread(cc_low[a]) * (here - spread(rim_low[k, q, a]))
+            for j in range(TILES):
+                at = pl.ds(8 * j, 8)
+                if j + 1 < TILES:
+                    after = v[q, a, 8 * j + 8 : 8 * j + 16, :]
+                    after_up = pltpu.roll(after, 7, 0)
+                else:
+                    after = None
+                    after_up = spread(rim_up[k, q, a])
+                flux_cross = cond[1, a, at, :] * (jnp.where(last_row, after_up, here_up) - here)
+                arrived = pltpu.roll(flux_cross, 1, 0)
+                flux_depth = cond[2, a, at, :] * (pltpu.roll(here, NC - 1, 1) - here)
+                flux_slab = cond[0, a, at, :] * (above(at) - here)
+                image = sto[a, at, :] * here
+                image = image - flux_slab + flux[at, :]
+                image = image - flux_cross + jnp.where(first_row, passed, arrived)
+                image = image - flux_depth + pltpu.roll(flux_depth, 1, 1)
+                flux[at, :] = flux_slab
+                w[q, a, at, :] = image
+                if k + 1 < ITERS:
+                    if j == 0:
+                        edge_low[k + 1, q, a] = image[0:1, :]
+                    if j == TILES - 1:
+                        edge_up[k + 1, q, a] = image[7:8, :]
+                dots = (dots[0] + fold(here * image), dots[1] + fold(image * image)) + (
+                    (dots[2] + fold(here * here),) if k == 0 else ()
+                )
+                passed, here, here_up = arrived, after, after_up
+            return dots
+
+        def apply(q, unused):
+            for copy in halo_copies(k, q):
+                copy.wait_recv()
+            for j in range(TILES):
+                at = pl.ds(8 * j, 8)
+                flux[at, :] = cs_low[at, :] * (v[q, 0, at, :] - halo_low[k, q, at, :])
+            dots = (jnp.zeros((8, 128), F32),) * (3 if k == 0 else 2)
+            dots = lax.fori_loop(
+                0, LA - 1,
+                lambda a, carry: layer(q, a, lambda at: v[q, a + 1, at, :], carry),
+                dots)
+            dots = layer(q, LA - 1, lambda at: halo_up[k, q, at, :], dots)
+            if k + 1 < ITERS:
+                for copy in halo_copies(k + 1, q):
+                    copy.start()
+            places = (2 * k + 1, 2 * k + 2, 0)
+            for place, dot in zip(places, dots):
+                moments[q, place : place + 1, :] = jnp.sum(dot, axis=0, keepdims=True)
+            return unused
+
+        lax.fori_loop(0, RHS, apply, 0)
+
+    rows = lax.broadcasted_iota(jnp.int32, (8, 128), 0)
+    lanes = lax.broadcasted_iota(jnp.int32, (8, 128), 1)
+    packed = jnp.zeros((8, 128), F32)
+    for q in range(RHS):
+        lane_sum = jnp.sum(moments[q], axis=1, keepdims=True)
+        packed = packed + jnp.where(lanes == rows + 8 * q, lane_sum, 0.0)
+    own = jnp.sum(packed, axis=0, keepdims=True)
+
+    for sent, got, group, place, index in (
+        (sent1, got1, group1, in_row, 0),
+        (sent2, got2, group2, row_y * 4 + c, 1),
+    ):
+        sent[...] = own
+        for peer in group:
+            pltpu.make_async_remote_copy(
+                src_ref=sent, dst_ref=got.at[place], send_sem=sum_send.at[index],
+                recv_sem=sum_recv.at[index], device_id=peer, device_id_type=MESH).start()
+        got[place] = own
+        others = got.at[pl.ds(0, len(group))]
+        pltpu.make_async_copy(others, others, sum_recv.at[index]).wait()
+        terms = [got[i] for i in range(len(group) + 1)]
+        while len(terms) > 1:
+            terms = [terms[i] + terms[i + 1] for i in range(0, len(terms), 2)]
+        own = terms[0]
+
+    summed = jnp.broadcast_to(own, (8, 128))
+    used = (lanes % 8 == 0) & (lanes < 8 * RHS)
+    stand_in = (1.0, 1.0, 2.0, 6.0, 24.0, 120.0, 720.0)
+    m = [
+        jnp.where(used, pltpu.roll(summed, (128 - j) % 128, 1) if j else summed, stand_in[j])
+        for j in range(7)
+    ]
+    coefs, sound = scalars_of(m)
+    for i, coef in enumerate(coefs):
+        coef_ref[i : i + 1, :] = coef[0:1, :]
+    coef_ref[6:8, :] = jnp.zeros((2, 128), F32)
+    sound_ref[...] = jnp.min(jnp.where(sound, 1, 0), axis=1, keepdims=True)[0:1, :]
+
+    for copy in cond_copies:
+        copy.wait_send()
+
+    def finish(q, unused):
+        for k in range(ITERS):
+            for copy in halo_copies(k, q):
+                copy.wait_send()
+        return unused
+
+    lax.fori_loop(0, RHS, finish, 0)
+    for got, group, index in ((got1, group1, 0), (got2, group2, 1)):
+        others = got.at[pl.ds(0, len(group))]
+        pltpu.make_async_copy(others, others, sum_send.at[index]).wait()
+
+
+def combine_kernel(coef, v0, v1, v2, v3, x_hbm, r_hbm, x, r, sem):
+    copies = []
+    for q in range(RHS):
+        x0, x1, x2, d1, d2, d3 = (coef[i, 8 * q] for i in range(6))
+
+        def layer(a, carry):
+            for j in range(TILES):
+                at = pl.ds(8 * j, 8)
+                t0, t1, t2, t3 = (v[q, a, at, :] for v in (v0, v1, v2, v3))
+                x[q, a, at, :] = x0 * t0 + x1 * t1 + x2 * t2
+                r[q, a, at, :] = t0 + d1 * t1 + d2 * t2 + d3 * t3
+            return carry
+
+        lax.fori_loop(0, LA, layer, 0)
+        for index, (source, target) in enumerate(((x, x_hbm), (r, r_hbm))):
+            copy = pltpu.make_async_copy(source.at[q], target.at[q], sem.at[q, index])
+            copy.start()
+            copies.append(copy)
+    for copy in copies:
+        copy.wait()
+
+
+def per_device(pressure_drive, throat_radius, wet_flag, cap_pressure, storage):
+    field = (RHS, LA, LB, NC)
+    vmem = functools.partial(pltpu.VMEM, dtype=F32)
+    in_vmem = pl.BlockSpec(memory_space=pltpu.VMEM)
+    anywhere = pl.BlockSpec(memory_space=pl.ANY)
+    *vectors, coefs, sound = pl.pallas_call(
+        powers_kernel,
+        out_shape=[pltpu.VMEM(field, F32)] * 4
+        + [jax.ShapeDtypeStruct((8, 128), F32), jax.ShapeDtypeStruct((1, 1), jnp.int32)],
+        in_specs=[anywhere] * 5,
+        out_specs=[in_vmem] * 6,
+        scratch_shapes=[
+            vmem(field),
+            pltpu.VMEM(field, jnp.int32),
+            vmem((LA, LB, NC)),
+            vmem((LA, LB, NC)),
+            vmem((LB, NC)),
+            vmem((LA, 1, NC)),
+            vmem((LA, 1, NC)),
+            vmem((ITERS, RHS, LB, NC)),
+            vmem((ITERS, RHS, LB, NC)),
+            vmem((ITERS, RHS, LA, 1, NC)),
+            vmem((ITERS, RHS, LA, 1, NC)),
+            vmem((ITERS, RHS, LA, 1, NC)),
+            vmem((ITERS, RHS, LA, 1, NC)),
+            vmem((LB, NC)),
+            vmem((RHS, 8, 128)),
+            vmem((1, 128)),
+            vmem((1, 128)),
+            vmem((8, 1, 128)),
+            vmem((16, 1, 128)),
+            pltpu.SemaphoreType.DMA((5,)),
+            pltpu.SemaphoreType.DMA((ITERS, RHS, 4)),
+            pltpu.SemaphoreType.DMA((ITERS, RHS, 4)),
+            pltpu.SemaphoreType.DMA((2,)),
+            pltpu.SemaphoreType.DMA((2,)),
+            pltpu.SemaphoreType.DMA((2,)),
+            pltpu.SemaphoreType.DMA((2,)),
+        ],
+        compiler_params=pltpu.CompilerParams(
+            collective_id=0, has_side_effects=True, vmem_limit_bytes=34 << 20
+        ),
+        name="powers",
+    )(pressure_drive, throat_radius, wet_flag, cap_pressure, storage)
+    fast = pl.pallas_call(
+        combine_kernel,
+        out_shape=[jax.ShapeDtypeStruct(field, F32)] * 2,
+        in_specs=[pl.BlockSpec(memory_space=pltpu.SMEM)] + [in_vmem] * 4,
+        out_specs=[anywhere] * 2,
+        scratch_shapes=[vmem(field), vmem(field), pltpu.SemaphoreType.DMA((RHS, 2))],
+        compiler_params=pltpu.CompilerParams(vmem_limit_bytes=24 << 20),
+        name="combine",
+    )(coefs, *vectors)
+    return lax.cond(
+        sound[0, 0] == 1,
+        lambda: tuple(fast),
+        lambda: plain_iteration(pressure_drive, throat_radius, wet_flag, cap_pressure, storage),
+    )
+
+
 def solution(mesh):
     in_specs = (
         P(None, "slab", "cross", None),

time: 454 us -> 46.4 us (0.10)
  blocking collectives: 329 us -> 0 us
  other arithmetic: 57.2 us -> 0 us
  Pallas kernels: 0 us -> 44.4 us
  starting transfers between devices: 38 us -> 0 us
  waiting for transfers between devices: 15.3 us -> 0 us
  local copies, waits for them, and re-layouts: 12 us -> 0.01 us
    psum x5 -> x0, blocking collectives: 329 us -> none  [the longest x3 196 us: squares(): return lax.psum(totals(residual * residual), ('slab', 'cross'))]
    pallas_call x0 -> x2, Pallas kernels: none -> 44.4 us  [the longest x1 40.6 us: per_device(): pl.pallas_call(powers_kernel, out_shape=[pltpu.VMEM(field, F32)] * 4 + [j...]
    ppermute x14 -> x0, starting transfers between devices: 38 us -> none  [the longest x6 20.3 us: with_halo(): lax.ppermute(tail, axis, [(i, (i + 1) % count) for i in range(ends)])]
    reduce_sum x5 -> x0, other arithmetic: 33.4 us -> none  [totals(): return jnp.sum(values, axis=(1, 2, 3))]
    ppermute x14 -> x0, waiting for transfers between devices: 15.3 us -> none  [the longest x6 9.7 us: with_halo(): lax.ppermute(head, axis, [((i + 1) % count, i) for i in range(ends)])]
    sub x1 -> x0, other arithmetic: 10 us -> none  [per_device(): residual = residual - widen(step_size) * applied]
    slice x10 -> x0, local copies, waits for them, and re-layouts: 9.3 us -> none  [the longest x3 6.85 us: depth_terms(): upper_values = jnp.pad(vector[..., 1:], ((0, 0), (0, 0), (0, 0), (0, 1)))]
    add x2 -> x0, other arithmetic: 6.39 us -> none  [per_device(): direction = residual + widen(norm_next / norm_now) * direction]
  transfers between devices with their start and end apart: 14 -> 0, of which waited for: 6 -> 0; matrix products, arithmetic and copies ran while one was open for 3% -> 0% of each run, Pallas kernels for 0% -> 0%
where the time goes in v1:
time: 46.4 us; the launch traced here: 46.1 us
  Pallas kernels  44.4 us (96%)
  between operations  1.51 us (3%)
    pallas_call x1, Pallas kernels, per_device(): pl.pallas_call(powers_kernel, out_shape=[pltpu.VMEM(field, F32)] * 4 + [j...  40.6 us
    pallas_call x1, Pallas kernels, per_device(): pl.pallas_call(combine_kernel, out_shape=[jax.ShapeDtypeStruct(field, F32...  3.73 us

profile of v1, /device:TPU:1, one launch (start us, length us, event | category | flops | bytes accessed | tf_op | source)
XLA Modules:
  0.0 46.1 jit_solution(7122733092558450165)
XLA Ops:
  0.6 0.0 copy-start
  0.6 40.6 %powers.1 = (f32[3,8,64,512]{3,2,1,0:T(8,128)S(1)}, f32[3,8,64,512]{3,2,1,0:T(8,128)S(1)}, f32[3,8,64,512]{3,2,1,0:T(8,128)S(1)}, f32[3,8,64,512]{3,2,1,0:T(8,12...) custom-call(f32[3,8,64,512]{3,2,1,0:T(8,128)} %b_hbm.1, f32[3,8,64,512]{3,2,1,0:T(8,128)} %rad_hbm.1, ...), custom_call_target="tpu_custom_call" | custom-call | tf_op jit(solution)/shard_map/powers/pallas_call | solution.py:433
  41.9 0.0 copy-done
  42.0 3.7 %combine.1 = (f32[3,8,64,512]{3,2,1,0:T(8,128)}, f32[3,8,64,512]{3,2,1,0:T(8,128)}) custom-call(f32[8,128]{1,0:T(8,128)S(1)} %get-tuple-element.28.coef, f32[3,8,64,512]{3,2,1,0:T(8,128)S(1)} %get-tuple-element.29.v0, f32[3,8,64,512]{3,2,1,0:T(8,128)S(1)} %get-tuple-element.30.v1, f32[3,8,64,512]{3,2,1,0:T(8,128)S(1)} %get-tuple-element.31.v2, ...), custom_call_target="tpu_custom_call" | custom-call | tf_op jit(solution)/shard_map/combine/pallas_call | solution.py:472
  45.7 0.2 conditional.1
Async XLA Ops:
  0.6 41.3 %copy-start = (f32[3,8,64,512]{3,2,1,0:T(8,128)S(1)}, f32[3,8,64,512]{3,2,1,0:T(8,128)}, u32[]{:S(2)}) copy-start(f32[3,8,64,512]{3,2,1,0:T(8,128)} %b_hbm.1) | copy-start | bytes 9437188

commit v2 on v1

--- a/solution.py
+++ b/solution.py
@@ -14,6 +14,7 @@
 SLABS, CROSSES = 32, 4
 LA, LB, NC = 8, 64, 512
 TILES = LB // 8
+CHUNKS = LA // 2
 ERROR_GAIN_MAX = 2500.0
 CANCEL_MAX = 300.0
 
@@ -186,8 +187,8 @@
     v0, v1, v2, v3, coef_ref, sound_ref,
     cond, wet, cap, sto, cs_low, cc_out, cc_low,
     halo_low, halo_up, edge_low, edge_up, rim_low, rim_up,
-    flux, moments, sent1, sent2, got1, got2,
-    load_sem, halo_send, halo_recv, cond_send, cond_recv, sum_send, sum_recv,
+    flux, dots_ref, sent1, sent2, got1, got2,
+    load_sem, chunk_sem, halo_send, halo_recv, cond_send, cond_recv, sum_send, sum_recv,
 ):
     s, c = lax.axis_index("slab"), lax.axis_index("cross")
     up, down = lax.rem(s + 1, SLABS), lax.rem(s + SLABS - 1, SLABS)
@@ -205,23 +206,61 @@
     for peer in greeted:
         pl.semaphore_signal(barrier, inc=1, device_id=peer, device_id_type=MESH)
 
-    loads = [
-        pltpu.make_async_copy(rad_hbm, cond, load_sem.at[0]),
-        pltpu.make_async_copy(wet_hbm, wet, load_sem.at[1]),
-        pltpu.make_async_copy(cap_hbm, cap, load_sem.at[2]),
-        pltpu.make_async_copy(b_hbm, v0, load_sem.at[3]),
-        pltpu.make_async_copy(sto_hbm, sto, load_sem.at[4]),
-    ]
-    for load in loads:
-        load.start()
-    for load in loads[:3]:
-        load.wait()
+    def chunk_copies(i):
+        layers = pl.ds(LA - 2 - 2 * i, 2)
+        return (
+            pltpu.make_async_copy(rad_hbm.at[:, layers], cond.at[:, layers], chunk_sem.at[i, 0]),
+            pltpu.make_async_copy(wet_hbm.at[:, layers], wet.at[:, layers], chunk_sem.at[i, 1]),
+            pltpu.make_async_copy(cap_hbm.at[layers], cap.at[layers], chunk_sem.at[i, 2]),
+        )
+
+    load_b = pltpu.make_async_copy(b_hbm, v0, load_sem.at[0])
+    load_sto = pltpu.make_async_copy(sto_hbm, sto, load_sem.at[1])
+    for i in range(CHUNKS):
+        for copy in chunk_copies(i):
+            copy.start()
+        if i == 0:
+            load_b.start()
+    load_sto.start()
+
+    vectors = (v0, v1, v2, v3)
+
+    def send(src, dst, k, q, place, device):
+        return pltpu.make_async_remote_copy(
+            src_ref=src, dst_ref=dst, send_sem=halo_send.at[k, q, place],
+            recv_sem=halo_recv.at[k, q, place], device_id=device, device_id_type=MESH)
+
+    def to_down(k, q):
+        src = b_hbm if k == 0 else vectors[k]
+        return send(src.at[q, 0], halo_up.at[k, q], k, q, 0, (down, c))
+
+    def to_up(k, q):
+        src = b_hbm if k == 0 else vectors[k]
+        return send(src.at[q, LA - 1], halo_low.at[k, q], k, q, 1, (up, c))
+
+    def to_left(k, q):
+        return send(edge_low.at[k, q], rim_up.at[k, q], k, q, 2, (s, left))
+
+    def to_right(k, q):
+        return send(edge_up.at[k, q], rim_low.at[k, q], k, q, 3, (s, right))
+
+    send_cs = pltpu.make_async_remote_copy(
+        src_ref=cond.at[0, LA - 1], dst_ref=cs_low, send_sem=cond_send.at[0],
+        recv_sem=cond_recv.at[0], device_id=(up, c), device_id_type=MESH)
+    send_cc = pltpu.make_async_remote_copy(
+        src_ref=cc_out, dst_ref=cc_low, send_sem=cond_send.at[1],
+        recv_sem=cond_recv.at[1], device_id=(s, right), device_id_type=MESH)
+
+    pl.semaphore_wait(barrier, len(greeted))
+    to_up(0, 0).start()
+    for q in range(RHS):
+        to_down(0, q).start()
 
     row = lax.broadcasted_iota(jnp.int32, (8, NC), 0)
     lane = lax.broadcasted_iota(jnp.int32, (8, NC), 1)
     first_row, last_row, last_lane = row == 0, row == 7, lane == NC - 1
 
-    def conduct(a, carry):
+    def conduct(a):
         ends_slab = (s == SLABS - 1) & (a == LA - 1)
         for j in range(TILES):
             at = pl.ds(8 * j, 8)
@@ -239,122 +278,162 @@
                 if k == 2:
                     value = jnp.where(last_lane, 0.0, value)
                 cond[k, a, at, :] = value
-        return carry
-
-    lax.fori_loop(0, LA, conduct, 0)
-
-    loads[3].wait()
-    for q in range(RHS):
-        for a in range(LA):
+
+    for copy in chunk_copies(0):
+        copy.wait()
+    conduct(LA - 1)
+    send_cs.start()
+    for q in range(1, RHS):
+        to_up(0, q).start()
+    load_b.wait()
+
+    def pack(a, carry):
+        for q in range(RHS):
             edge_low[0, q, a] = v0[q, a, 0:1, :]
             edge_up[0, q, a] = v0[q, a, LB - 1 : LB, :]
-    loads[4].wait()
-    moments[...] = jnp.zeros_like(moments)
-    pl.semaphore_wait(barrier, len(greeted))
-
-    vectors = (v0, v1, v2, v3)
-
-    def halo_copies(k, q):
-        v = vectors[k]
-        return (
-            pltpu.make_async_remote_copy(
-                src_ref=v.at[q, 0], dst_ref=halo_up.at[k, q], send_sem=halo_send.at[k, q, 0],
-                recv_sem=halo_recv.at[k, q, 0], device_id=(down, c), device_id_type=MESH),
-            pltpu.make_async_remote_copy(
-                src_ref=v.at[q, LA - 1], dst_ref=halo_low.at[k, q], send_sem=halo_send.at[k, q, 1],
-                recv_sem=halo_recv.at[k, q, 1], device_id=(up, c), device_id_type=MESH),
-            pltpu.make_async_remote_copy(
-                src_ref=edge_low.at[k, q], dst_ref=rim_up.at[k, q], send_sem=halo_send.at[k, q, 2],
-                recv_sem=halo_recv.at[k, q, 2], device_id=(s, left), device_id_type=MESH),
-            pltpu.make_async_remote_copy(
-                src_ref=edge_up.at[k, q], dst_ref=rim_low.at[k, q], send_sem=halo_send.at[k, q, 3],
-                recv_sem=halo_recv.at[k, q, 3], device_id=(s, right), device_id_type=MESH),
-        )
-
-    cond_copies = (
-        pltpu.make_async_remote_copy(
-            src_ref=cond.at[0, LA - 1], dst_ref=cs_low, send_sem=cond_send.at[0],
-            recv_sem=cond_recv.at[0], device_id=(up, c), device_id_type=MESH),
-        pltpu.make_async_remote_copy(
-            src_ref=cc_out, dst_ref=cc_low, send_sem=cond_send.at[1],
-            recv_sem=cond_recv.at[1], device_id=(s, right), device_id_type=MESH),
-    )
+        return carry
+
+    lax.fori_loop(0, LA, pack, 0)
     for q in range(RHS):
-        for copy in halo_copies(0, q):
-            copy.start()
-        if q == 0:
-            for copy in cond_copies:
-                copy.start()
-    for copy in cond_copies:
-        copy.wait_recv()
-
-    def spread(line):
-        return jnp.broadcast_to(line, (8, NC))
-
-    for k in range(ITERS):
+        to_left(0, q).start()
+        to_right(0, q).start()
+    conduct(LA - 2)
+
+    def chunk(i, carry):
+        for copy in chunk_copies(i):
+            copy.wait()
+        conduct(LA - 1 - 2 * i)
+        conduct(LA - 2 - 2 * i)
+        return carry
+
+    lax.fori_loop(1, CHUNKS, chunk, 0)
+    send_cc.start()
+    load_sto.wait()
+    dots_ref[...] = jnp.zeros_like(dots_ref)
+
+    def stages(k):
         v, w = vectors[k], vectors[k + 1]
-
-        def layer(q, a, above, carry):
-            dots = carry
+        places = (2 * k + 1, 2 * k + 2) + ((0,) if k == 0 else ())
+
+        def layer(q, a, below, above, keep, dots):
             here = v[q, a, 0:8, :]
             here_up = pltpu.roll(here, 7, 0)
-            passed = spread(cc_low[a]) * (here - spread(rim_low[k, q, a]))
+            passed = jnp.zeros((8, NC), F32)
             for j in range(TILES):
                 at = pl.ds(8 * j, 8)
                 if j + 1 < TILES:
                     after = v[q, a, 8 * j + 8 : 8 * j + 16, :]
                     after_up = pltpu.roll(after, 7, 0)
                 else:
-                    after = None
-                    after_up = spread(rim_up[k, q, a])
+                    after = after_up = here
                 flux_cross = cond[1, a, at, :] * (jnp.where(last_row, after_up, here_up) - here)
                 arrived = pltpu.roll(flux_cross, 1, 0)
                 flux_depth = cond[2, a, at, :] * (pltpu.roll(here, NC - 1, 1) - here)
                 flux_slab = cond[0, a, at, :] * (above(at) - here)
                 image = sto[a, at, :] * here
-                image = image - flux_slab + flux[at, :]
+                image = image - flux_slab + below(at, here)
                 image = image - flux_cross + jnp.where(first_row, passed, arrived)
                 image = image - flux_depth + pltpu.roll(flux_depth, 1, 1)
-                flux[at, :] = flux_slab
+                if keep:
+                    flux[at, :] = flux_slab
                 w[q, a, at, :] = image
-                if k + 1 < ITERS:
-                    if j == 0:
-                        edge_low[k + 1, q, a] = image[0:1, :]
-                    if j == TILES - 1:
-                        edge_up[k + 1, q, a] = image[7:8, :]
                 dots = (dots[0] + fold(here * image), dots[1] + fold(image * image)) + (
                     (dots[2] + fold(here * here),) if k == 0 else ()
                 )
                 passed, here, here_up = arrived, after, after_up
             return dots
 
-        def apply(q, unused):
-            for copy in halo_copies(k, q):
-                copy.wait_recv()
+        def interior(q, unused):
             for j in range(TILES):
                 at = pl.ds(8 * j, 8)
-                flux[at, :] = cs_low[at, :] * (v[q, 0, at, :] - halo_low[k, q, at, :])
-            dots = (jnp.zeros((8, 128), F32),) * (3 if k == 0 else 2)
+                flux[at, :] = cond[0, 0, at, :] * (v[q, 1, at, :] - v[q, 0, at, :])
+            dots = (jnp.zeros((8, 128), F32),) * len(places)
             dots = lax.fori_loop(
-                0, LA - 1,
-                lambda a, carry: layer(q, a, lambda at: v[q, a + 1, at, :], carry),
+                1, LA - 1,
+                lambda a, carry: layer(
+                    q, a, lambda at, here: flux[at, :], lambda at: v[q, a + 1, at, :], True, carry),
                 dots)
-            dots = layer(q, LA - 1, lambda at: halo_up[k, q, at, :], dots)
+            for place, dot in zip(places, dots):
+                dots_ref[q, place] = dot
+            return unused
+
+        def rim(q, a, dots):
+            low, high = edge_low[k, q, a], edge_up[k, q, a]
+            enters = cc_low[a] * (low - rim_low[k, q, a])
+            leaves = cc_out[a] * (rim_up[k, q, a] - high)
+            first, last = w[q, a, 0:1, :], w[q, a, LB - 1 : LB, :]
+            new_first, new_last = first + enters, last - leaves
+            w[q, a, 0:1, :] = new_first
+            w[q, a, LB - 1 : LB, :] = new_last
             if k + 1 < ITERS:
-                for copy in halo_copies(k + 1, q):
-                    copy.start()
-            places = (2 * k + 1, 2 * k + 2, 0)
-            for place, dot in zip(places, dots):
-                moments[q, place : place + 1, :] = jnp.sum(dot, axis=0, keepdims=True)
+                edge_low[k + 1, q, a] = new_first
+                edge_up[k + 1, q, a] = new_last
+            return (
+                dots[0] + fold(low * enters - high * leaves),
+                dots[1] + fold(enters * (first + new_first) - leaves * (last + new_last)),
+            )
+
+        def border(q, unused):
+            to_down(k, q).wait_recv()
+            to_left(k, q).wait_recv()
+            to_right(k, q).wait_recv()
+            if k == 0:
+                @pl.when(q == 0)
+                def _():
+                    send_cc.wait_recv()
+            dots = (jnp.zeros((8, 128), F32),) * len(places)
+            line = (jnp.zeros((1, 128), F32),) * 2
+            dots = layer(
+                q, LA - 1,
+                lambda at, here: cond[0, LA - 2, at, :] * (here - v[q, LA - 2, at, :]),
+                lambda at: halo_up[k, q, at, :], False, dots)
+            line = rim(q, LA - 1, line)
+            if k + 1 < ITERS:
+                to_up(k + 1, q).start()
+            to_up(k, q).wait_recv()
+            if k == 0:
+                @pl.when(q == 0)
+                def _():
+                    send_cs.wait_recv()
+            dots = layer(
+                q, 0,
+                lambda at, here: cs_low[at, :] * (here - halo_low[k, q, at, :]),
+                lambda at: v[q, 1, at, :], False, dots)
+            line = rim(q, 0, line)
+            if k + 1 < ITERS:
+                to_down(k + 1, q).start()
+            line = lax.fori_loop(1, LA - 1, lambda a, carry: rim(q, a, carry), line)
+            if k + 1 < ITERS:
+                to_left(k + 1, q).start()
+                to_right(k + 1, q).start()
+            for i, (place, dot) in enumerate(zip(places, dots)):
+                dots_ref[q, place] = dots_ref[q, place] + dot
+                if i < 2:
+                    dots_ref[q, place, 0:1, :] = dots_ref[q, place, 0:1, :] + line[i]
             return unused
 
-        lax.fori_loop(0, RHS, apply, 0)
+        return interior, border
+
+    interior, border = stages(0)
+    lax.fori_loop(0, RHS, interior, 0)
+    for k in range(1, ITERS):
+        next_interior, next_border = stages(k)
+
+        def both(q, unused, border=border, interior=next_interior):
+            border(q, unused)
+            return interior(q, unused)
+
+        lax.fori_loop(0, RHS, both, 0)
+        border = next_border
+    lax.fori_loop(0, RHS, border, 0)
 
     rows = lax.broadcasted_iota(jnp.int32, (8, 128), 0)
     lanes = lax.broadcasted_iota(jnp.int32, (8, 128), 1)
     packed = jnp.zeros((8, 128), F32)
     for q in range(RHS):
-        lane_sum = jnp.sum(moments[q], axis=1, keepdims=True)
+        moments = jnp.concatenate(
+            [jnp.sum(dots_ref[q, j], axis=0, keepdims=True) for j in range(8)], axis=0)
+        lane_sum = jnp.sum(moments, axis=1, keepdims=True)
         packed = packed + jnp.where(lanes == rows + 8 * q, lane_sum, 0.0)
     own = jnp.sum(packed, axis=0, keepdims=True)
 
@@ -388,12 +467,12 @@
     coef_ref[6:8, :] = jnp.zeros((2, 128), F32)
     sound_ref[...] = jnp.min(jnp.where(sound, 1, 0), axis=1, keepdims=True)[0:1, :]
 
-    for copy in cond_copies:
-        copy.wait_send()
+    send_cs.wait_send()
+    send_cc.wait_send()
 
     def finish(q, unused):
         for k in range(ITERS):
-            for copy in halo_copies(k, q):
+            for copy in (to_down(k, q), to_up(k, q), to_left(k, q), to_right(k, q)):
                 copy.wait_send()
         return unused
 
@@ -404,6 +483,7 @@
 
 
 def combine_kernel(coef, v0, v1, v2, v3, x_hbm, r_hbm, x, r, sem):
+    half = LA // 2
     copies = []
     for q in range(RHS):
         x0, x1, x2, d1, d2, d3 = (coef[i, 8 * q] for i in range(6))
@@ -416,11 +496,14 @@
                 r[q, a, at, :] = t0 + d1 * t1 + d2 * t2 + d3 * t3
             return carry
 
-        lax.fori_loop(0, LA, layer, 0)
-        for index, (source, target) in enumerate(((x, x_hbm), (r, r_hbm))):
-            copy = pltpu.make_async_copy(source.at[q], target.at[q], sem.at[q, index])
-            copy.start()
-            copies.append(copy)
+        for h in range(2):
+            lax.fori_loop(h * half, (h + 1) * half, layer, 0)
+            part = pl.ds(h * half, half)
+            for index, (source, target) in enumerate(((x, x_hbm), (r, r_hbm))):
+                copy = pltpu.make_async_copy(
+                    source.at[q, part], target.at[q, part], sem.at[q, h, index])
+                copy.start()
+                copies.append(copy)
     for copy in copies:
         copy.wait()
 
@@ -451,12 +534,13 @@
             vmem((ITERS, RHS, LA, 1, NC)),
             vmem((ITERS, RHS, LA, 1, NC)),
             vmem((LB, NC)),
-            vmem((RHS, 8, 128)),
+            vmem((RHS, 8, 8, 128)),
             vmem((1, 128)),
             vmem((1, 128)),
             vmem((8, 1, 128)),
             vmem((16, 1, 128)),
-            pltpu.SemaphoreType.DMA((5,)),
+            pltpu.SemaphoreType.DMA((2,)),
+            pltpu.SemaphoreType.DMA((CHUNKS, 3)),
             pltpu.SemaphoreType.DMA((ITERS, RHS, 4)),
             pltpu.SemaphoreType.DMA((ITERS, RHS, 4)),
             pltpu.SemaphoreType.DMA((2,)),
@@ -474,7 +558,7 @@
         out_shape=[jax.ShapeDtypeStruct(field, F32)] * 2,
         in_specs=[pl.BlockSpec(memory_space=pltpu.SMEM)] + [in_vmem] * 4,
         out_specs=[anywhere] * 2,
-        scratch_shapes=[vmem(field), vmem(field), pltpu.SemaphoreType.DMA((RHS, 2))],
+        scratch_shapes=[vmem(field), vmem(field), pltpu.SemaphoreType.DMA((RHS, 2, 2))],
         compiler_params=pltpu.CompilerParams(vmem_limit_bytes=24 << 20),
         name="combine",
     )(coefs, *vectors)

time: 46.4 us -> 42.2 us (0.909)
  Pallas kernels: 44.4 us -> 40.1 us
    pallas_call x1, Pallas kernels: 40.6 us -> 36.6 us  [per_device(): pl.pallas_call(powers_kernel, out_shape=[pltpu.VMEM(field, F32)] * 4 + [j...]
where the time goes in v2:
time: 42.2 us; the launch traced here: 41.9 us
  Pallas kernels  40.1 us (95%)
  between operations  1.51 us (4%)
    pallas_call x1, Pallas kernels, per_device(): pl.pallas_call(powers_kernel, out_shape=[pltpu.VMEM(field, F32)] * 4 + [j...  36.6 us
    pallas_call x1, Pallas kernels, per_device(): pl.pallas_call(combine_kernel, out_shape=[jax.ShapeDtypeStruct(field, F32...  3.56 us

profile of v2, /device:TPU:1, one launch (start us, length us, event | category | flops | bytes accessed | tf_op | source)
XLA Modules:
  0.0 41.9 jit_solution(2548406467575320196)
XLA Ops:
  0.6 0.0 copy-start
  0.6 36.6 %powers.1 = (f32[3,8,64,512]{3,2,1,0:T(8,128)S(1)}, f32[3,8,64,512]{3,2,1,0:T(8,128)S(1)}, f32[3,8,64,512]{3,2,1,0:T(8,128)S(1)}, f32[3,8,64,512]{3,2,1,0:T(8,12...) custom-call(f32[3,8,64,512]{3,2,1,0:T(8,128)} %b_hbm.1, f32[3,8,64,512]{3,2,1,0:T(8,128)} %rad_hbm.1, ...), custom_call_target="tpu_custom_call" | custom-call | tf_op jit(solution)/shard_map/powers/pallas_call | solution.py:516
  37.9 0.0 copy-done
  37.9 3.6 %combine.1 = (f32[3,8,64,512]{3,2,1,0:T(8,128)}, f32[3,8,64,512]{3,2,1,0:T(8,128)}) custom-call(f32[8,128]{1,0:T(8,128)S(1)} %get-tuple-element.28.coef, f32[3,8,64,512]{3,2,1,0:T(8,128)S(1)} %get-tuple-element.29.v0, f32[3,8,64,512]{3,2,1,0:T(8,128)S(1)} %get-tuple-element.30.v1, f32[3,8,64,512]{3,2,1,0:T(8,128)S(1)} %get-tuple-element.31.v2, ...), custom_call_target="tpu_custom_call" | custom-call | tf_op jit(solution)/shard_map/combine/pallas_call | solution.py:556
  41.5 0.2 conditional.1
Async XLA Ops:
  0.6 37.3 %copy-start = (f32[3,8,64,512]{3,2,1,0:T(8,128)S(1)}, f32[3,8,64,512]{3,2,1,0:T(8,128)}, u32[]{:S(2)}) copy-start(f32[3,8,64,512]{3,2,1,0:T(8,128)} %b_hbm.1) | copy-start | bytes 9437188

commit v3 on v2

--- a/solution.py
+++ b/solution.py
@@ -15,8 +15,15 @@
 LA, LB, NC = 8, 64, 512
 TILES = LB // 8
 CHUNKS = LA // 2
-ERROR_GAIN_MAX = 2500.0
-CANCEL_MAX = 300.0
+CHIP_OFFSETS = sorted(
+    [(y, z, x) for y in range(4) for z in range(4) for x in range(4) if x or y or z],
+    key=lambda offset: -sum(min(step, 4 - step) for step in offset),
+)
+ERROR_GAIN_MAX = 3000.0
+CANCEL_MAX = 150.0
+MOMENTS = 6
+PAIRS = [(i, j) for i in range(4) for j in range(i, 4)]
+LANES = MOMENTS + len(PAIRS)
 
 
 def shifted(value, axis, steps):
@@ -104,7 +111,7 @@
     return (solution, residual)
 
 
-def scalars_of(m):
+def scalars_of(m, sample):
     def parts(c0, c1, c2, first):
         return (
             c0 * c0 * m[first],
@@ -117,9 +124,6 @@
 
     def total(terms):
         return (terms[0] + terms[1]) + (terms[2] + terms[3]) + (terms[4] + terms[5])
-
-    def bulk(terms):
-        return total([jnp.abs(term) for term in terms])
 
     rr0 = m[0]
     step0 = m[0] / m[1]
@@ -147,24 +151,21 @@
     x2 = step2 * q2
     d1, d2, d3 = r1 - step2 * q0, r2 - step2 * q1, -step2 * q2
 
-    image2 = parts(q0, q1, q2, 2)
-    rr3 = step2 * step2 * total(image2) - rr2
+    d = (1.0, d1, d2, d3)
+    rr3 = 0.0
+    for products, (i, j) in zip(sample, PAIRS):
+        rr3 = rr3 + (1.0 if i == j else 2.0) * d[i] * d[j] * products
     gain1 = (image0 + rr0) / rr1
     gain2 = (energy1[0] + jnp.abs(energy1[1]) + energy1[2]) / curve1
     gain3 = (step1 * step1 * (image1[0] + jnp.abs(image1[1]) + image1[2]) + rr1) / rr2
-    gain4 = bulk(energy2) / curve2
-    gain5 = (step2 * step2 * bulk(image2) + rr2) / rr3
+    gain4 = total([jnp.abs(term) for term in energy2]) / curve2
     gain = (
         (gain1 + gain2) * jnp.sqrt(rr0 / rr3)
         + gain3 * jnp.sqrt(rr1 / rr3)
-        + gain4 * jnp.sqrt(rr2 / rr3)
-        + gain5
+        + gain4 * jnp.sqrt((rr2 + rr3) / rr3)
     )
     cancel = (
-        jnp.sqrt(m[0])
-        + jnp.abs(d1) * jnp.sqrt(m[2])
-        + jnp.abs(d2) * jnp.sqrt(m[4])
-        + jnp.abs(d3) * jnp.sqrt(m[6])
+        jnp.sqrt(m[0]) + jnp.abs(d1) * jnp.sqrt(m[2]) + jnp.abs(d2) * jnp.sqrt(m[4])
     ) / jnp.sqrt(rr3)
     sound = (
         (rr1 > 0.0)
@@ -186,25 +187,29 @@
     b_hbm, rad_hbm, wet_hbm, cap_hbm, sto_hbm,
     v0, v1, v2, v3, coef_ref, sound_ref,
     cond, wet, cap, sto, cs_low, cc_out, cc_low,
-    halo_low, halo_up, edge_low, edge_up, rim_low, rim_up,
-    flux, dots_ref, sent1, sent2, got1, got2,
-    load_sem, chunk_sem, halo_send, halo_recv, cond_send, cond_recv, sum_send, sum_recv,
+    halo_low, halo_up, edge_low, edge_up, rims,
+    flux, dots_ref, early_sum, token, met, sent, got, pair_sent, pair_got,
+    load_sem, chunk_sem, halo_send, halo_recv, cond_send, cond_recv, meet_send, meet_recv,
+    sum_send, sum_recv,
 ):
     s, c = lax.axis_index("slab"), lax.axis_index("cross")
-    up, down = lax.rem(s + 1, SLABS), lax.rem(s + SLABS - 1, SLABS)
-    right, left = lax.rem(c + 1, CROSSES), lax.rem(c + CROSSES - 1, CROSSES)
-    row_y, in_row = s // 8, lax.rem(s, 8)
-    group1 = [(row_y * 8 + lax.rem(in_row + i, 8), c) for i in range(1, 8)]
-    group2 = [
-        (lax.rem(row_y + i, 4) * 8 + in_row, lax.rem(c + j, 4))
-        for i in range(4)
-        for j in range(4)
-        if i or j
-    ]
+    has_up, has_down = s < SLABS - 1, s > 0
+    has_right, has_left = c < CROSSES - 1, c > 0
+    up, down = jnp.where(has_up, s + 1, s - 1), jnp.where(has_down, s - 1, s + 1)
+    right, left = jnp.where(has_right, c + 1, c - 1), jnp.where(has_left, c - 1, c + 1)
+    row_y = s // 8
+    col_z, core = lax.rem(s // 2, 4), lax.rem(s, 2)
+    along_z = [(row_y * 8 + lax.rem(col_z + i, 4) * 2 + core, c) for i in range(1, 4)]
+    along_y = [(lax.rem(row_y + i, 4) * 8 + lax.rem(s, 8), c) for i in range(1, 4)]
+    along_x = [(s, lax.rem(c + i, 4)) for i in range(1, 4)]
     barrier = pltpu.get_barrier_semaphore()
-    greeted = [(up, c), (down, c), (s, right), (s, left)] + group1 + group2
+    greeted = along_x + along_z + along_y
     for peer in greeted:
         pl.semaphore_signal(barrier, inc=1, device_id=peer, device_id_type=MESH)
+    for there, peer in ((has_up, up), (has_down, down)):
+        @pl.when(there)
+        def _(peer=peer):
+            pl.semaphore_signal(barrier, inc=1, device_id=(peer, c), device_id_type=MESH)
 
     def chunk_copies(i):
         layers = pl.ds(LA - 2 - 2 * i, 2)
@@ -225,24 +230,43 @@
 
     vectors = (v0, v1, v2, v3)
 
-    def send(src, dst, k, q, place, device):
+    def send(src, dst, direction, arrival, device):
         return pltpu.make_async_remote_copy(
-            src_ref=src, dst_ref=dst, send_sem=halo_send.at[k, q, place],
-            recv_sem=halo_recv.at[k, q, place], device_id=device, device_id_type=MESH)
+            src_ref=src, dst_ref=dst, send_sem=halo_send.at[direction], recv_sem=arrival,
+            device_id=device, device_id_type=MESH)
 
     def to_down(k, q):
         src = b_hbm if k == 0 else vectors[k]
-        return send(src.at[q, 0], halo_up.at[k, q], k, q, 0, (down, c))
+        return send(src.at[q, 0], halo_up.at[k, q], 0, halo_recv.at[k, q, 0], (down, c))
 
     def to_up(k, q):
         src = b_hbm if k == 0 else vectors[k]
-        return send(src.at[q, LA - 1], halo_low.at[k, q], k, q, 1, (up, c))
-
-    def to_left(k, q):
-        return send(edge_low.at[k, q], rim_up.at[k, q], k, q, 2, (s, left))
-
-    def to_right(k, q):
-        return send(edge_up.at[k, q], rim_low.at[k, q], k, q, 3, (s, right))
+        return send(src.at[q, LA - 1], halo_low.at[k, q], 1, halo_recv.at[k, q, 1], (up, c))
+
+    def to_sides(k, q):
+        arrival = halo_recv.at[k, q, 2]
+
+        @pl.when(has_left)
+        def _():
+            send(edge_low.at[k, q], rims.at[k, q, 1], 2, arrival, (s, left)).start()
+
+        @pl.when(has_right)
+        def _():
+            send(edge_up.at[k, q], rims.at[k, q, 0], 3, arrival, (s, right)).start()
+
+    def wait_sides(k, q):
+        arrival = halo_recv.at[k, q, 2]
+
+        @pl.when(has_left & has_right)
+        def _():
+            wait_for(rims.at[k, q], arrival)
+
+        @pl.when(jnp.logical_not(has_left & has_right))
+        def _():
+            wait_for(rims.at[k, q, 0], arrival)
+
+    def wait_for(whole, sem):
+        pltpu.make_async_copy(whole, whole, sem).wait()
 
     send_cs = pltpu.make_async_remote_copy(
         src_ref=cond.at[0, LA - 1], dst_ref=cs_low, send_sem=cond_send.at[0],
@@ -251,10 +275,40 @@
         src_ref=cc_out, dst_ref=cc_low, send_sem=cond_send.at[1],
         recv_sem=cond_recv.at[1], device_id=(s, right), device_id_type=MESH)
 
-    pl.semaphore_wait(barrier, len(greeted))
-    to_up(0, 0).start()
-    for q in range(RHS):
-        to_down(0, q).start()
+    pl.semaphore_wait(barrier, len(greeted) + jnp.where(has_up & has_down, 2, 1))
+
+    def start_up(copies):
+        @pl.when(has_up)
+        def _():
+            for copy in copies():
+                copy.start()
+
+    def start_down(copies):
+        @pl.when(has_down)
+        def _():
+            for copy in copies():
+                copy.start()
+
+    start_up(lambda: [to_up(0, 0)])
+    start_down(lambda: [to_down(0, q) for q in range(RHS)])
+
+    @pl.when(s == 0)
+    def _():
+        halo_low[...] = jnp.zeros_like(halo_low)
+        cs_low[...] = jnp.zeros_like(cs_low)
+
+    @pl.when(s == SLABS - 1)
+    def _():
+        halo_up[...] = jnp.zeros_like(halo_up)
+
+    @pl.when(c == 0)
+    def _():
+        rims[:, :, 0] = jnp.zeros((ITERS, RHS, LA, 1, NC), F32)
+        cc_low[...] = jnp.zeros_like(cc_low)
+
+    @pl.when(c == CROSSES - 1)
+    def _():
+        rims[:, :, 1] = jnp.zeros((ITERS, RHS, LA, 1, NC), F32)
 
     row = lax.broadcasted_iota(jnp.int32, (8, NC), 0)
     lane = lax.broadcasted_iota(jnp.int32, (8, NC), 1)
@@ -282,9 +336,8 @@
     for copy in chunk_copies(0):
         copy.wait()
     conduct(LA - 1)
-    send_cs.start()
-    for q in range(1, RHS):
-        to_up(0, q).start()
+    start_up(lambda: [send_cs] + [to_up(0, q) for q in range(1, RHS)])
+    token[...] = jnp.zeros_like(token)
     load_b.wait()
 
     def pack(a, carry):
@@ -295,8 +348,7 @@
 
     lax.fori_loop(0, LA, pack, 0)
     for q in range(RHS):
-        to_left(0, q).start()
-        to_right(0, q).start()
+        to_sides(0, q)
     conduct(LA - 2)
 
     def chunk(i, carry):
@@ -307,15 +359,20 @@
         return carry
 
     lax.fori_loop(1, CHUNKS, chunk, 0)
-    send_cc.start()
+
+    @pl.when(has_right)
+    def _():
+        send_cc.start()
+
     load_sto.wait()
     dots_ref[...] = jnp.zeros_like(dots_ref)
 
     def stages(k):
         v, w = vectors[k], vectors[k + 1]
-        places = (2 * k + 1, 2 * k + 2) + ((0,) if k == 0 else ())
-
-        def layer(q, a, below, above, keep, dots):
+        last = k + 1 == ITERS
+        places = ((1, 2, 0), (3, 4), (5,))[k]
+
+        def layer(q, a, below, above, keep, dots, faces=False):
             here = v[q, a, 0:8, :]
             here_up = pltpu.roll(here, 7, 0)
             passed = jnp.zeros((8, NC), F32)
@@ -329,25 +386,36 @@
                 flux_cross = cond[1, a, at, :] * (jnp.where(last_row, after_up, here_up) - here)
                 arrived = pltpu.roll(flux_cross, 1, 0)
                 flux_depth = cond[2, a, at, :] * (pltpu.roll(here, NC - 1, 1) - here)
-                flux_slab = cond[0, a, at, :] * (above(at) - here)
+                higher = above(at)
+                flux_slab = cond[0, a, at, :] * (higher - here)
                 image = sto[a, at, :] * here
-                image = image - flux_slab + below(at, here)
+                image = image - flux_slab
+                if below is not None:
+                    image = image + below(at, here)
                 image = image - flux_cross + jnp.where(first_row, passed, arrived)
                 image = image - flux_depth + pltpu.roll(flux_depth, 1, 1)
                 if keep:
                     flux[at, :] = flux_slab
                 w[q, a, at, :] = image
-                dots = (dots[0] + fold(here * image), dots[1] + fold(image * image)) + (
-                    (dots[2] + fold(here * here),) if k == 0 else ()
-                )
+                products = [here * image]
+                if faces:
+                    products[0] = products[0] + higher * flux_slab
+                if k + 1 < ITERS:
+                    products.append(image * image)
+                if k == 0:
+                    products.append(here * here)
+                dots = tuple(dot + fold(product) for dot, product in zip(dots, products))
                 passed, here, here_up = arrived, after, after_up
             return dots
 
         def interior(q, unused):
-            for j in range(TILES):
-                at = pl.ds(8 * j, 8)
-                flux[at, :] = cond[0, 0, at, :] * (v[q, 1, at, :] - v[q, 0, at, :])
             dots = (jnp.zeros((8, 128), F32),) * len(places)
+            if last:
+                dots = layer(q, 0, None, lambda at: v[q, 1, at, :], True, dots)
+            else:
+                for j in range(TILES):
+                    at = pl.ds(8 * j, 8)
+                    flux[at, :] = cond[0, 0, at, :] * (v[q, 1, at, :] - v[q, 0, at, :])
             dots = lax.fori_loop(
                 1, LA - 1,
                 lambda a, carry: layer(
@@ -357,65 +425,121 @@
                 dots_ref[q, place] = dot
             return unused
 
-        def rim(q, a, dots):
-            low, high = edge_low[k, q, a], edge_up[k, q, a]
-            enters = cc_low[a] * (low - rim_low[k, q, a])
-            leaves = cc_out[a] * (rim_up[k, q, a] - high)
-            first, last = w[q, a, 0:1, :], w[q, a, LB - 1 : LB, :]
-            new_first, new_last = first + enters, last - leaves
-            w[q, a, 0:1, :] = new_first
-            w[q, a, LB - 1 : LB, :] = new_last
-            if k + 1 < ITERS:
-                edge_low[k + 1, q, a] = new_first
-                edge_up[k + 1, q, a] = new_last
+        def rim_first(q, a, line):
+            low = edge_low[k, q, a]
+            enters = cc_low[a] * (low - rims[k, q, 0, a])
+            old = w[q, a, 0:1, :]
+            new = old + enters
+            w[q, a, 0:1, :] = new
+            if last:
+                return (line[0] + fold(low * enters),)
+            edge_low[k + 1, q, a] = new
+            return line[0] + fold(low * enters), line[1] + fold(enters * (old + new))
+
+        def rim_last(q, a, line):
+            high = edge_up[k, q, a]
+            leaves = cc_out[a] * (rims[k, q, 1, a] - high)
+            old = w[q, a, LB - 1 : LB, :]
+            new = old - leaves
+            w[q, a, LB - 1 : LB, :] = new
+            if last:
+                return (line[0] - fold(high * leaves),)
+            edge_up[k + 1, q, a] = new
+            return line[0] - fold(high * leaves), line[1] - fold(leaves * (old + new))
+
+        def below_top(q):
+            return lambda at, here: cond[0, LA - 2, at, :] * (here - v[q, LA - 2, at, :])
+
+        def below_bottom(q):
+            return lambda at, here: cs_low[at, :] * (here - halo_low[k, q, at, :])
+
+        def only_first(q, there, wait):
+            if k == 0:
+                @pl.when((q == 0) & there)
+                def _():
+                    wait()
+
+        def both_rims(q, a, line):
+            return rim_last(q, a, rim_first(q, a, line))
+
+        def no_dots():
             return (
-                dots[0] + fold(low * enters - high * leaves),
-                dots[1] + fold(enters * (first + new_first) - leaves * (last + new_last)),
+                (jnp.zeros((8, 128), F32),) * len(places),
+                (jnp.zeros((1, 128), F32),) * min(2, len(places)),
             )
 
-        def border(q, unused):
-            to_down(k, q).wait_recv()
-            to_left(k, q).wait_recv()
-            to_right(k, q).wait_recv()
-            if k == 0:
-                @pl.when(q == 0)
-                def _():
-                    send_cc.wait_recv()
-            dots = (jnp.zeros((8, 128), F32),) * len(places)
-            line = (jnp.zeros((1, 128), F32),) * 2
-            dots = layer(
-                q, LA - 1,
-                lambda at, here: cond[0, LA - 2, at, :] * (here - v[q, LA - 2, at, :]),
-                lambda at: halo_up[k, q, at, :], False, dots)
-            line = rim(q, LA - 1, line)
-            if k + 1 < ITERS:
-                to_up(k + 1, q).start()
-            to_up(k, q).wait_recv()
-            if k == 0:
-                @pl.when(q == 0)
-                def _():
-                    send_cs.wait_recv()
-            dots = layer(
-                q, 0,
-                lambda at, here: cs_low[at, :] * (here - halo_low[k, q, at, :]),
-                lambda at: v[q, 1, at, :], False, dots)
-            line = rim(q, 0, line)
-            if k + 1 < ITERS:
-                to_down(k + 1, q).start()
-            line = lax.fori_loop(1, LA - 1, lambda a, carry: rim(q, a, carry), line)
-            if k + 1 < ITERS:
-                to_left(k + 1, q).start()
-                to_right(k + 1, q).start()
+        def add_dots(q, dots, line):
             for i, (place, dot) in enumerate(zip(places, dots)):
                 dots_ref[q, place] = dots_ref[q, place] + dot
-                if i < 2:
+                if i < len(line):
                     dots_ref[q, place, 0:1, :] = dots_ref[q, place, 0:1, :] + line[i]
+
+        def top(q):
+            dots, line = no_dots()
+            @pl.when(has_up)
+            def _():
+                to_down(k, q).wait_recv()
+
+            dots = layer(
+                q, LA - 1, below_top(q), lambda at: halo_up[k, q, at, :], False, dots, last)
+            line = both_rims(q, LA - 1, line)
+            if not last:
+                start_up(lambda: [to_up(k + 1, q)])
+            add_dots(q, dots, line)
+
+        def bottom(q):
+            dots, line = no_dots()
+
+            @pl.when(has_down)
+            def _():
+                to_up(k, q).wait_recv()
+
+            only_first(q, has_down, lambda: send_cs.wait_recv())
+            dots = layer(q, 0, below_bottom(q), lambda at: v[q, 1, at, :], False, dots)
+            line = both_rims(q, 0, line)
+            start_down(lambda: [to_down(k + 1, q)])
+            add_dots(q, dots, line)
+
+        def inner_rims(q, low):
+            line = lax.fori_loop(
+                low, LA - 1, lambda a, carry: both_rims(q, a, carry), no_dots()[1])
+            add_dots(q, no_dots()[0], line)
+
+        def border(q, unused):
+            wait_sides(k, q)
+            only_first(q, has_left, lambda: send_cc.wait_recv())
+            if last:
+                inner_rims(q, 0)
+                top(q)
+                return unused
+
+            @pl.when(core == 0)
+            def _():
+                bottom(q)
+                top(q)
+
+            @pl.when(core == 1)
+            def _():
+                top(q)
+                bottom(q)
+
+            inner_rims(q, 1)
+            to_sides(k + 1, q)
             return unused
 
         return interior, border
 
+    def step(index, group):
+        for i, peer in enumerate(group):
+            pltpu.make_async_remote_copy(
+                src_ref=token, dst_ref=met.at[index, i], send_sem=meet_send.at[index],
+                recv_sem=meet_recv.at[index], device_id=peer, device_id_type=MESH).start()
+
+    step(0, along_z)
     interior, border = stages(0)
     lax.fori_loop(0, RHS, interior, 0)
+    wait_for(met.at[0], meet_recv.at[0])
+    step(1, along_y)
     for k in range(1, ITERS):
         next_interior, next_border = stages(k)
 
@@ -425,68 +549,132 @@
 
         lax.fori_loop(0, RHS, both, 0)
         border = next_border
-    lax.fori_loop(0, RHS, border, 0)
+        if k == 1:
+            wait_for(met.at[1], meet_recv.at[1])
+            step(2, along_x)
+        else:
+            wait_for(met.at[2], meet_recv.at[2])
+
+    def sample_products(q, unused):
+        def line(a, sums):
+            for j in range(1, TILES - 1):
+                at = pl.ds(8 * j, 8)
+                t = [vector[q, a, at, :] for vector in vectors]
+                sums = tuple(
+                    total + fold(t[i] * t[l]) for total, (i, l) in zip(sums, PAIRS))
+            return sums
+
+        sums = lax.fori_loop(2, LA - 2, line, (jnp.zeros((8, 128), F32),) * len(PAIRS))
+        for place, total in enumerate(sums):
+            dots_ref[q, MOMENTS + place] = total
+        return unused
+
+    lax.fori_loop(0, RHS, sample_products, 0)
 
     rows = lax.broadcasted_iota(jnp.int32, (8, 128), 0)
     lanes = lax.broadcasted_iota(jnp.int32, (8, 128), 1)
-    packed = jnp.zeros((8, 128), F32)
+
+    def lane_sums(tiles, target):
+        stacked = jnp.concatenate(
+            [jnp.sum(tile, axis=0, keepdims=True) for tile in tiles], axis=0)
+        spread = jnp.broadcast_to(jnp.sum(stacked, axis=1, keepdims=True), (8, 128))
+        return jnp.where(lanes == target, spread, 0.0)
+
+    early = jnp.zeros((8, 128), F32)
     for q in range(RHS):
-        moments = jnp.concatenate(
-            [jnp.sum(dots_ref[q, j], axis=0, keepdims=True) for j in range(8)], axis=0)
-        lane_sum = jnp.sum(moments, axis=1, keepdims=True)
-        packed = packed + jnp.where(lanes == rows + 8 * q, lane_sum, 0.0)
+        tiles = [dots_ref[q, j] for j in range(LANES) if j != MOMENTS - 1]
+        tiles.append(jnp.zeros((8, 128), F32))
+        early = early + lane_sums(tiles[:8], LANES * q + rows + jnp.where(rows >= 5, 1, 0))
+        early = early + lane_sums(tiles[8:], LANES * q + rows + 9)
+    early_sum[...] = early
+
+    lax.fori_loop(0, RHS, border, 0)
+
+    late = [dots_ref[min(q, RHS - 1), MOMENTS - 1] for q in range(8)]
+    packed = early_sum[...] + jnp.where(
+        rows < RHS, lane_sums(late, LANES * rows + MOMENTS - 1), 0.0)
     own = jnp.sum(packed, axis=0, keepdims=True)
 
-    for sent, got, group, place, index in (
-        (sent1, got1, group1, in_row, 0),
-        (sent2, got2, group2, row_y * 4 + c, 1),
-    ):
-        sent[...] = own
-        for peer in group:
-            pltpu.make_async_remote_copy(
-                src_ref=sent, dst_ref=got.at[place], send_sem=sum_send.at[index],
-                recv_sem=sum_recv.at[index], device_id=peer, device_id_type=MESH).start()
-        got[place] = own
-        others = got.at[pl.ds(0, len(group))]
-        pltpu.make_async_copy(others, others, sum_recv.at[index]).wait()
-        terms = [got[i] for i in range(len(group) + 1)]
-        while len(terms) > 1:
-            terms = [terms[i] + terms[i + 1] for i in range(0, len(terms), 2)]
-        own = terms[0]
+    chip = (row_y * 4 + col_z) * 4 + c
+    sent[...] = own
+    for dy, dz, dx in CHIP_OFFSETS:
+        slab = lax.rem(row_y + dy, 4) * 8 + lax.rem(col_z + dz, 4) * 2 + core
+        pltpu.make_async_remote_copy(
+            src_ref=sent, dst_ref=got.at[chip], send_sem=sum_send.at[0],
+            recv_sem=sum_recv.at[0], device_id=(slab, lax.rem(c + dx, 4)),
+            device_id_type=MESH).start()
+    got[chip] = own
+
+    def complete(q, unused):
+        @pl.when(has_down)
+        def _():
+            to_up(ITERS - 1, q).wait_recv()
+
+        for j in range(TILES):
+            at = pl.ds(8 * j, 8)
+            v3[q, 0, at, :] = v3[q, 0, at, :] + cs_low[at, :] * (
+                v2[q, 0, at, :] - halo_low[ITERS - 1, q, at, :])
+        return unused
+
+    lax.fori_loop(0, RHS, complete, 0)
+
+    @pl.when(has_down)
+    def _():
+        wait_for(halo_up, halo_send.at[0])
+
+    @pl.when(has_up)
+    def _():
+        wait_for(halo_low, halo_send.at[1])
+        send_cs.wait_send()
+
+    @pl.when(has_left)
+    def _():
+        wait_for(edge_low, halo_send.at[2])
+
+    @pl.when(has_right)
+    def _():
+        wait_for(edge_up, halo_send.at[3])
+        send_cc.wait_send()
+
+    for index in range(3):
+        wait_for(met.at[index], meet_send.at[index])
+
+    others = got.at[pl.ds(0, len(CHIP_OFFSETS))]
+    wait_for(others, sum_recv.at[0])
+    terms = [got[i] for i in range(len(CHIP_OFFSETS) + 1)]
+    while len(terms) > 1:
+        terms = [terms[i] + terms[i + 1] for i in range(0, len(terms), 2)]
+    pair_sent[...] = terms[0]
+    pair = pltpu.make_async_remote_copy(
+        src_ref=pair_sent, dst_ref=pair_got, send_sem=sum_send.at[1], recv_sem=sum_recv.at[1],
+        device_id=(s + 1 - 2 * core, c), device_id_type=MESH)
+    pair.start()
+    wait_for(others, sum_send.at[0])
+    pair.wait_recv()
+    own = terms[0] + pair_got[...]
 
     summed = jnp.broadcast_to(own, (8, 128))
-    used = (lanes % 8 == 0) & (lanes < 8 * RHS)
-    stand_in = (1.0, 1.0, 2.0, 6.0, 24.0, 120.0, 720.0)
+    used = (lanes % LANES == 0) & (lanes < LANES * RHS)
+    stand_in = (1.0, 1.0, 2.0, 6.0, 24.0, 120.0) + (1.0,) * len(PAIRS)
     m = [
-        jnp.where(used, pltpu.roll(summed, (128 - j) % 128, 1) if j else summed, stand_in[j])
-        for j in range(7)
+        jnp.where(used, pltpu.roll(summed, 128 - j, 1) if j else summed, stand_in[j])
+        for j in range(LANES)
     ]
-    coefs, sound = scalars_of(m)
+    coefs, sound = scalars_of(m[:MOMENTS], m[MOMENTS:])
+    sound = sound | ~used
     for i, coef in enumerate(coefs):
         coef_ref[i : i + 1, :] = coef[0:1, :]
     coef_ref[6:8, :] = jnp.zeros((2, 128), F32)
     sound_ref[...] = jnp.min(jnp.where(sound, 1, 0), axis=1, keepdims=True)[0:1, :]
 
-    send_cs.wait_send()
-    send_cc.wait_send()
-
-    def finish(q, unused):
-        for k in range(ITERS):
-            for copy in (to_down(k, q), to_up(k, q), to_left(k, q), to_right(k, q)):
-                copy.wait_send()
-        return unused
-
-    lax.fori_loop(0, RHS, finish, 0)
-    for got, group, index in ((got1, group1, 0), (got2, group2, 1)):
-        others = got.at[pl.ds(0, len(group))]
-        pltpu.make_async_copy(others, others, sum_send.at[index]).wait()
+    pair.wait_send()
 
 
 def combine_kernel(coef, v0, v1, v2, v3, x_hbm, r_hbm, x, r, sem):
-    half = LA // 2
+    part = 2
     copies = []
     for q in range(RHS):
-        x0, x1, x2, d1, d2, d3 = (coef[i, 8 * q] for i in range(6))
+        x0, x1, x2, d1, d2, d3 = (coef[i, LANES * q] for i in range(6))
 
         def layer(a, carry):
             for j in range(TILES):
@@ -496,12 +684,12 @@
                 r[q, a, at, :] = t0 + d1 * t1 + d2 * t2 + d3 * t3
             return carry
 
-        for h in range(2):
-            lax.fori_loop(h * half, (h + 1) * half, layer, 0)
-            part = pl.ds(h * half, half)
+        for h in range(LA // part):
+            lax.fori_loop(h * part, (h + 1) * part, layer, 0)
+            layers = pl.ds(h * part, part)
             for index, (source, target) in enumerate(((x, x_hbm), (r, r_hbm))):
                 copy = pltpu.make_async_copy(
-                    source.at[q, part], target.at[q, part], sem.at[q, h, index])
+                    source.at[q, layers], target.at[q, layers], sem.at[q, h, index])
                 copy.start()
                 copies.append(copy)
     for copy in copies:
@@ -531,20 +719,24 @@
             vmem((ITERS, RHS, LB, NC)),
             vmem((ITERS, RHS, LA, 1, NC)),
             vmem((ITERS, RHS, LA, 1, NC)),
-            vmem((ITERS, RHS, LA, 1, NC)),
-            vmem((ITERS, RHS, LA, 1, NC)),
+            vmem((ITERS, RHS, 2, LA, 1, NC)),
             vmem((LB, NC)),
-            vmem((RHS, 8, 8, 128)),
+            vmem((RHS, LANES, 8, 128)),
+            vmem((8, 128)),
+            vmem((1, 128)),
+            vmem((3, 3, 1, 128)),
+            vmem((1, 128)),
+            vmem((64, 1, 128)),
             vmem((1, 128)),
             vmem((1, 128)),
-            vmem((8, 1, 128)),
-            vmem((16, 1, 128)),
             pltpu.SemaphoreType.DMA((2,)),
             pltpu.SemaphoreType.DMA((CHUNKS, 3)),
-            pltpu.SemaphoreType.DMA((ITERS, RHS, 4)),
-            pltpu.SemaphoreType.DMA((ITERS, RHS, 4)),
+            pltpu.SemaphoreType.DMA((4,)),
+            pltpu.SemaphoreType.DMA((ITERS, RHS, 3)),
             pltpu.SemaphoreType.DMA((2,)),
             pltpu.SemaphoreType.DMA((2,)),
+            pltpu.SemaphoreType.DMA((3,)),
+            pltpu.SemaphoreType.DMA((3,)),
             pltpu.SemaphoreType.DMA((2,)),
             pltpu.SemaphoreType.DMA((2,)),
         ],
@@ -558,7 +750,7 @@
         out_shape=[jax.ShapeDtypeStruct(field, F32)] * 2,
         in_specs=[pl.BlockSpec(memory_space=pltpu.SMEM)] + [in_vmem] * 4,
         out_specs=[anywhere] * 2,
-        scratch_shapes=[vmem(field), vmem(field), pltpu.SemaphoreType.DMA((RHS, 2, 2))],
+        scratch_shapes=[vmem(field), vmem(field), pltpu.SemaphoreType.DMA((RHS, 4, 2))],
         compiler_params=pltpu.CompilerParams(vmem_limit_bytes=24 << 20),
         name="combine",
     )(coefs, *vectors)

time: 42.2 us -> 41.6 us (0.986)
  no operation moved by 1% of the time
where the time goes in v3:
time: 41.6 us; the launch traced here: 41.5 us
  Pallas kernels  39.7 us (95%)
  between operations  1.51 us (4%)
    pallas_call x1, Pallas kernels, per_device(): pl.pallas_call(powers_kernel, out_shape=[pltpu.VMEM(field, F32)] * 4 + [j...  36.2 us
    pallas_call x1, Pallas kernels, per_device(): pl.pallas_call(combine_kernel, out_shape=[jax.ShapeDtypeStruct(field, F32...  3.54 us

profile of v3, /device:TPU:1, one launch (start us, length us, event | category | flops | bytes accessed | tf_op | source)
XLA Modules:
  0.0 41.5 jit_solution(1941345280632347240)
XLA Ops:
  0.6 0.0 copy-start
  0.6 36.2 %powers.1 = (f32[3,8,64,512]{3,2,1,0:T(8,128)S(1)}, f32[3,8,64,512]{3,2,1,0:T(8,128)S(1)}, f32[3,8,64,512]{3,2,1,0:T(8,128)S(1)}, f32[3,8,64,512]{3,2,1,0:T(8,12...) custom-call(f32[3,8,64,512]{3,2,1,0:T(8,128)} %b_hbm.1, f32[3,8,64,512]{3,2,1,0:T(8,128)} %rad_hbm.1, ...), custom_call_target="tpu_custom_call" | custom-call | tf_op jit(solution)/shard_map/powers/pallas_call | solution.py:704
  37.5 0.0 copy-done
  37.5 3.5 %combine.1 = (f32[3,8,64,512]{3,2,1,0:T(8,128)}, f32[3,8,64,512]{3,2,1,0:T(8,128)}) custom-call(f32[8,128]{1,0:T(8,128)S(1)} %get-tuple-element.28.coef, f32[3,8,64,512]{3,2,1,0:T(8,128)S(1)} %get-tuple-element.29.v0, f32[3,8,64,512]{3,2,1,0:T(8,128)S(1)} %get-tuple-element.30.v1, f32[3,8,64,512]{3,2,1,0:T(8,128)S(1)} %get-tuple-element.31.v2, ...), custom_call_target="tpu_custom_call" | custom-call | tf_op jit(solution)/shard_map/combine/pallas_call | solution.py:748
  41.1 0.2 conditional.1
Async XLA Ops:
  0.6 36.9 %copy-start = (f32[3,8,64,512]{3,2,1,0:T(8,128)S(1)}, f32[3,8,64,512]{3,2,1,0:T(8,128)}, u32[]{:S(2)}) copy-start(f32[3,8,64,512]{3,2,1,0:T(8,128)} %b_hbm.1) | copy-start | bytes 9437188

commit v4 on v3

--- a/solution.py
+++ b/solution.py
@@ -663,8 +663,9 @@
     coefs, sound = scalars_of(m[:MOMENTS], m[MOMENTS:])
     sound = sound | ~used
     for i, coef in enumerate(coefs):
-        coef_ref[i : i + 1, :] = coef[0:1, :]
-    coef_ref[6:8, :] = jnp.zeros((2, 128), F32)
+        for q in range(RHS):
+            mine = jnp.where(lanes == LANES * q, coef, 0.0)
+            coef_ref[q, i] = jnp.broadcast_to(jnp.sum(mine, axis=1, keepdims=True), (8, 128))
     sound_ref[...] = jnp.min(jnp.where(sound, 1, 0), axis=1, keepdims=True)[0:1, :]
 
     pair.wait_send()
@@ -674,7 +675,8 @@
     part = 2
     copies = []
     for q in range(RHS):
-        x0, x1, x2, d1, d2, d3 = (coef[i, LANES * q] for i in range(6))
+        x0, x1, x2, d1, d2, d3 = (
+            jnp.concatenate([coef[q, i]] * (NC // 128), axis=1) for i in range(6))
 
         def layer(a, carry):
             for j in range(TILES):
@@ -704,7 +706,10 @@
     *vectors, coefs, sound = pl.pallas_call(
         powers_kernel,
         out_shape=[pltpu.VMEM(field, F32)] * 4
-        + [jax.ShapeDtypeStruct((8, 128), F32), jax.ShapeDtypeStruct((1, 1), jnp.int32)],
+        + [
+            pltpu.VMEM((RHS, 6, 8, 128), F32),
+            jax.ShapeDtypeStruct((1, 1), jnp.int32),
+        ],
         in_specs=[anywhere] * 5,
         out_specs=[in_vmem] * 6,
         scratch_shapes=[
@@ -748,7 +753,7 @@
     fast = pl.pallas_call(
         combine_kernel,
         out_shape=[jax.ShapeDtypeStruct(field, F32)] * 2,
-        in_specs=[pl.BlockSpec(memory_space=pltpu.SMEM)] + [in_vmem] * 4,
+        in_specs=[in_vmem] * 5,
         out_specs=[anywhere] * 2,
         scratch_shapes=[vmem(field), vmem(field), pltpu.SemaphoreType.DMA((RHS, 4, 2))],
         compiler_params=pltpu.CompilerParams(vmem_limit_bytes=24 << 20),

time: 41.6 us -> 41 us (0.986)
  Pallas kernels: 39.7 us -> 39.1 us
    pallas_call x1, Pallas kernels: 3.54 us -> 2.94 us  [per_device(): pl.pallas_call(combine_kernel, out_shape=[jax.ShapeDtypeStruct(field, F32...]
where the time goes in v4:
time: 41 us; the launch traced here: 40.9 us
  Pallas kernels  39.1 us (95%)
  between operations  1.51 us (4%)
    pallas_call x1, Pallas kernels, per_device(): pl.pallas_call(powers_kernel, out_shape=[pltpu.VMEM(field, F32)] * 4 + [p...  36.2 us
    pallas_call x1, Pallas kernels, per_device(): pl.pallas_call(combine_kernel, out_shape=[jax.ShapeDtypeStruct(field, F32...  2.94 us

profile of v4, /device:TPU:1, one launch (start us, length us, event | category | flops | bytes accessed | tf_op | source)
XLA Modules:
  0.0 40.9 jit_solution(9217992078739220776)
XLA Ops:
  0.6 0.0 copy-start
  0.6 36.2 %powers.1 = (f32[3,8,64,512]{3,2,1,0:T(8,128)S(1)}, f32[3,8,64,512]{3,2,1,0:T(8,128)S(1)}, f32[3,8,64,512]{3,2,1,0:T(8,128)S(1)}, f32[3,8,64,512]{3,2,1,0:T(8,12...) custom-call(f32[3,8,64,512]{3,2,1,0:T(8,128)} %b_hbm.1, f32[3,8,64,512]{3,2,1,0:T(8,128)} %rad_hbm.1, ...), custom_call_target="tpu_custom_call" | custom-call | tf_op jit(solution)/shard_map/powers/pallas_call | solution.py:706
  37.5 0.0 copy-done
  37.5 2.9 %combine.1 = (f32[3,8,64,512]{3,2,1,0:T(8,128)}, f32[3,8,64,512]{3,2,1,0:T(8,128)}) custom-call(f32[3,6,8,128]{3,2,1,0:T(8,128)S(1)} %get-tuple-element.28.coef, f32[3,8,64,512]{3,2,1,0:T(8,128)S(1)} %get-tuple-element.29.v0, f32[3,8,64,512]{3,2,1,0:T(8,128)S(1)} %get-tuple-element.30.v1, f32[3,8,64,512]{3,2,1,0:T(8,128)S(1)} %get-tuple-element.31.v2, ...), custom_call_target="tpu_custom_call" | custom-call | tf_op jit(solution)/shard_map/combine/pallas_call | solution.py:753
  40.5 0.2 conditional.1
Async XLA Ops:
  0.6 36.9 %copy-start = (f32[3,8,64,512]{3,2,1,0:T(8,128)S(1)}, f32[3,8,64,512]{3,2,1,0:T(8,128)}, u32[]{:S(2)}) copy-start(f32[3,8,64,512]{3,2,1,0:T(8,128)} %b_hbm.1) | copy-start | bytes 9437188

commit v5 on v4

--- a/solution.py
+++ b/solution.py
@@ -372,7 +372,7 @@
         last = k + 1 == ITERS
         places = ((1, 2, 0), (3, 4), (5,))[k]
 
-        def layer(q, a, below, above, keep, dots, faces=False):
+        def layer(q, a, below, above, dots):
             here = v[q, a, 0:8, :]
             here_up = pltpu.roll(here, 7, 0)
             passed = jnp.zeros((8, NC), F32)
@@ -386,20 +386,17 @@
                 flux_cross = cond[1, a, at, :] * (jnp.where(last_row, after_up, here_up) - here)
                 arrived = pltpu.roll(flux_cross, 1, 0)
                 flux_depth = cond[2, a, at, :] * (pltpu.roll(here, NC - 1, 1) - here)
-                higher = above(at)
-                flux_slab = cond[0, a, at, :] * (higher - here)
                 image = sto[a, at, :] * here
-                image = image - flux_slab
-                if below is not None:
-                    image = image + below(at, here)
+                if below:
+                    image = image + flux[at, :]
+                if above:
+                    flux_slab = cond[0, a, at, :] * (v[q, a + 1, at, :] - here)
+                    image = image - flux_slab
+                    flux[at, :] = flux_slab
                 image = image - flux_cross + jnp.where(first_row, passed, arrived)
                 image = image - flux_depth + pltpu.roll(flux_depth, 1, 1)
-                if keep:
-                    flux[at, :] = flux_slab
                 w[q, a, at, :] = image
                 products = [here * image]
-                if faces:
-                    products[0] = products[0] + higher * flux_slab
                 if k + 1 < ITERS:
                     products.append(image * image)
                 if k == 0:
@@ -410,17 +407,10 @@
 
         def interior(q, unused):
             dots = (jnp.zeros((8, 128), F32),) * len(places)
-            if last:
-                dots = layer(q, 0, None, lambda at: v[q, 1, at, :], True, dots)
-            else:
-                for j in range(TILES):
-                    at = pl.ds(8 * j, 8)
-                    flux[at, :] = cond[0, 0, at, :] * (v[q, 1, at, :] - v[q, 0, at, :])
+            dots = layer(q, 0, False, True, dots)
             dots = lax.fori_loop(
-                1, LA - 1,
-                lambda a, carry: layer(
-                    q, a, lambda at, here: flux[at, :], lambda at: v[q, a + 1, at, :], True, carry),
-                dots)
+                1, LA - 1, lambda a, carry: layer(q, a, True, True, carry), dots)
+            dots = layer(q, LA - 1, True, False, dots)
             for place, dot in zip(places, dots):
                 dots_ref[q, place] = dot
             return unused
@@ -447,12 +437,6 @@
             edge_up[k + 1, q, a] = new
             return line[0] - fold(high * leaves), line[1] - fold(leaves * (old + new))
 
-        def below_top(q):
-            return lambda at, here: cond[0, LA - 2, at, :] * (here - v[q, LA - 2, at, :])
-
-        def below_bottom(q):
-            return lambda at, here: cs_low[at, :] * (here - halo_low[k, q, at, :])
-
         def only_first(q, there, wait):
             if k == 0:
                 @pl.when((q == 0) & there)
@@ -474,42 +458,58 @@
                 if i < len(line):
                     dots_ref[q, place, 0:1, :] = dots_ref[q, place, 0:1, :] + line[i]
 
+        def face(q, a, enters, energy):
+            dots = (jnp.zeros((8, 128), F32),) * min(2, len(places))
+            for j in range(TILES):
+                at = pl.ds(8 * j, 8)
+                flux_in = enters(at)
+                old = w[q, a, at, :]
+                new = old + flux_in
+                w[q, a, at, :] = new
+                dots = (dots[0] + fold(energy(at, flux_in)),) + (
+                    () if last else (dots[1] + fold(flux_in * (old + new)),)
+                )
+                if not last and j == 0:
+                    edge_low[k + 1, q, a] = new[0:1, :]
+                if not last and j == TILES - 1:
+                    edge_up[k + 1, q, a] = new[7:8, :]
+            return dots
+
         def top(q):
-            dots, line = no_dots()
             @pl.when(has_up)
             def _():
                 to_down(k, q).wait_recv()
 
-            dots = layer(
-                q, LA - 1, below_top(q), lambda at: halo_up[k, q, at, :], False, dots, last)
-            line = both_rims(q, LA - 1, line)
+            a = LA - 1
+            dots = face(
+                q, a,
+                lambda at: cond[0, a, at, :] * (v[q, a, at, :] - halo_up[k, q, at, :]),
+                lambda at, flux_in: flux_in * (
+                    v[q, a, at, :] - halo_up[k, q, at, :] if last else v[q, a, at, :]))
             if not last:
                 start_up(lambda: [to_up(k + 1, q)])
-            add_dots(q, dots, line)
+            add_dots(q, dots, ())
 
         def bottom(q):
-            dots, line = no_dots()
-
             @pl.when(has_down)
             def _():
                 to_up(k, q).wait_recv()
 
             only_first(q, has_down, lambda: send_cs.wait_recv())
-            dots = layer(q, 0, below_bottom(q), lambda at: v[q, 1, at, :], False, dots)
-            line = both_rims(q, 0, line)
+            dots = face(
+                q, 0,
+                lambda at: cs_low[at, :] * (v[q, 0, at, :] - halo_low[k, q, at, :]),
+                lambda at, flux_in: flux_in * v[q, 0, at, :])
             start_down(lambda: [to_down(k + 1, q)])
-            add_dots(q, dots, line)
-
-        def inner_rims(q, low):
-            line = lax.fori_loop(
-                low, LA - 1, lambda a, carry: both_rims(q, a, carry), no_dots()[1])
-            add_dots(q, no_dots()[0], line)
+            add_dots(q, dots, ())
 
         def border(q, unused):
             wait_sides(k, q)
             only_first(q, has_left, lambda: send_cc.wait_recv())
+            line = lax.fori_loop(
+                0, LA, lambda a, carry: both_rims(q, a, carry), no_dots()[1])
+            add_dots(q, no_dots()[0], line)
             if last:
-                inner_rims(q, 0)
                 top(q)
                 return unused
 
@@ -523,7 +523,6 @@
                 top(q)
                 bottom(q)
 
-            inner_rims(q, 1)
             to_sides(k + 1, q)
             return unused
 

time: 41 us -> 40.6 us (level)
    pallas_call x1, Pallas kernels: 36.2 us -> 35.7 us  [per_device(): pl.pallas_call(powers_kernel, out_shape=[pltpu.VMEM(field, F32)] * 4 + [p...]
where the time goes in v5:
time: 40.6 us; the launch traced here: 40.4 us
  Pallas kernels  38.7 us (95%)
  between operations  1.51 us (4%)
    pallas_call x1, Pallas kernels, per_device(): pl.pallas_call(powers_kernel, out_shape=[pltpu.VMEM(field, F32)] * 4 + [p...  35.7 us
    pallas_call x1, Pallas kernels, per_device(): pl.pallas_call(combine_kernel, out_shape=[jax.ShapeDtypeStruct(field, F32...  2.94 us

profile of v5, /device:TPU:1, one launch (start us, length us, event | category | flops | bytes accessed | tf_op | source)
XLA Modules:
  0.0 40.4 jit_solution(11344143404402480752)
XLA Ops:
  0.6 0.0 copy-start
  0.6 35.7 %powers.1 = (f32[3,8,64,512]{3,2,1,0:T(8,128)S(1)}, f32[3,8,64,512]{3,2,1,0:T(8,128)S(1)}, f32[3,8,64,512]{3,2,1,0:T(8,128)S(1)}, f32[3,8,64,512]{3,2,1,0:T(8,12...) custom-call(f32[3,8,64,512]{3,2,1,0:T(8,128)} %b_hbm.1, f32[3,8,64,512]{3,2,1,0:T(8,128)} %rad_hbm.1, ...), custom_call_target="tpu_custom_call" | custom-call | tf_op jit(solution)/shard_map/powers/pallas_call | solution.py:705
  37.1 0.0 copy-done
  37.1 2.9 %combine.1 = (f32[3,8,64,512]{3,2,1,0:T(8,128)}, f32[3,8,64,512]{3,2,1,0:T(8,128)}) custom-call(f32[3,6,8,128]{3,2,1,0:T(8,128)S(1)} %get-tuple-element.28.coef, f32[3,8,64,512]{3,2,1,0:T(8,128)S(1)} %get-tuple-element.29.v0, f32[3,8,64,512]{3,2,1,0:T(8,128)S(1)} %get-tuple-element.30.v1, f32[3,8,64,512]{3,2,1,0:T(8,128)S(1)} %get-tuple-element.31.v2, ...), custom_call_target="tpu_custom_call" | custom-call | tf_op jit(solution)/shard_map/combine/pallas_call | solution.py:752
  40.0 0.2 conditional.1
Async XLA Ops:
  0.6 36.4 %copy-start = (f32[3,8,64,512]{3,2,1,0:T(8,128)S(1)}, f32[3,8,64,512]{3,2,1,0:T(8,128)}, u32[]{:S(2)}) copy-start(f32[3,8,64,512]{3,2,1,0:T(8,128)} %b_hbm.1) | copy-start | bytes 9437188

commit v6 on v5

--- a/solution.py
+++ b/solution.py
@@ -15,9 +15,13 @@
 LA, LB, NC = 8, 64, 512
 TILES = LB // 8
 CHUNKS = LA // 2
-CHIP_OFFSETS = sorted(
-    [(y, z, x) for y in range(4) for z in range(4) for x in range(4) if x or y or z],
-    key=lambda offset: -sum(min(step, 4 - step) for step in offset),
+OFFSETS = sorted(
+    [
+        (y, z, x, core)
+        for y in range(4) for z in range(4) for x in range(4) for core in range(2)
+        if x or y or z or core
+    ],
+    key=lambda offset: -sum(min(step, 4 - step) for step in offset[:3]),
 )
 ERROR_GAIN_MAX = 3000.0
 CANCEL_MAX = 150.0
@@ -188,7 +192,7 @@
     v0, v1, v2, v3, coef_ref, sound_ref,
     cond, wet, cap, sto, cs_low, cc_out, cc_low,
     halo_low, halo_up, edge_low, edge_up, rims,
-    flux, dots_ref, early_sum, token, met, sent, got, pair_sent, pair_got,
+    flux, dots_ref, early_sum, token, met, sent, got,
     load_sem, chunk_sem, halo_send, halo_recv, cond_send, cond_recv, meet_send, meet_recv,
     sum_send, sum_recv,
 ):
@@ -594,15 +598,16 @@
         rows < RHS, lane_sums(late, LANES * rows + MOMENTS - 1), 0.0)
     own = jnp.sum(packed, axis=0, keepdims=True)
 
-    chip = (row_y * 4 + col_z) * 4 + c
+    own_place = s * CROSSES + c
     sent[...] = own
-    for dy, dz, dx in CHIP_OFFSETS:
-        slab = lax.rem(row_y + dy, 4) * 8 + lax.rem(col_z + dz, 4) * 2 + core
+    for dy, dz, dx, other in OFFSETS:
+        at_core = 1 - core if other else core
+        slab = lax.rem(row_y + dy, 4) * 8 + lax.rem(col_z + dz, 4) * 2 + at_core
         pltpu.make_async_remote_copy(
-            src_ref=sent, dst_ref=got.at[chip], send_sem=sum_send.at[0],
+            src_ref=sent, dst_ref=got.at[own_place], send_sem=sum_send.at[0],
             recv_sem=sum_recv.at[0], device_id=(slab, lax.rem(c + dx, 4)),
             device_id_type=MESH).start()
-    got[chip] = own
+    got[own_place] = own
 
     def complete(q, unused):
         @pl.when(has_down)
@@ -638,19 +643,13 @@
     for index in range(3):
         wait_for(met.at[index], meet_send.at[index])
 
-    others = got.at[pl.ds(0, len(CHIP_OFFSETS))]
+    others = got.at[pl.ds(0, len(OFFSETS))]
     wait_for(others, sum_recv.at[0])
-    terms = [got[i] for i in range(len(CHIP_OFFSETS) + 1)]
+    terms = [got[i] for i in range(len(OFFSETS) + 1)]
     while len(terms) > 1:
         terms = [terms[i] + terms[i + 1] for i in range(0, len(terms), 2)]
-    pair_sent[...] = terms[0]
-    pair = pltpu.make_async_remote_copy(
-        src_ref=pair_sent, dst_ref=pair_got, send_sem=sum_send.at[1], recv_sem=sum_recv.at[1],
-        device_id=(s + 1 - 2 * core, c), device_id_type=MESH)
-    pair.start()
+    own = terms[0]
     wait_for(others, sum_send.at[0])
-    pair.wait_recv()
-    own = terms[0] + pair_got[...]
 
     summed = jnp.broadcast_to(own, (8, 128))
     used = (lanes % LANES == 0) & (lanes < LANES * RHS)
@@ -666,8 +665,6 @@
             mine = jnp.where(lanes == LANES * q, coef, 0.0)
             coef_ref[q, i] = jnp.broadcast_to(jnp.sum(mine, axis=1, keepdims=True), (8, 128))
     sound_ref[...] = jnp.min(jnp.where(sound, 1, 0), axis=1, keepdims=True)[0:1, :]
-
-    pair.wait_send()
 
 
 def combine_kernel(coef, v0, v1, v2, v3, x_hbm, r_hbm, x, r, sem):
@@ -730,9 +727,7 @@
             vmem((1, 128)),
             vmem((3, 3, 1, 128)),
             vmem((1, 128)),
-            vmem((64, 1, 128)),
-            vmem((1, 128)),
-            vmem((1, 128)),
+            vmem((128, 1, 128)),
             pltpu.SemaphoreType.DMA((2,)),
             pltpu.SemaphoreType.DMA((CHUNKS, 3)),
             pltpu.SemaphoreType.DMA((4,)),
@@ -741,8 +736,8 @@
             pltpu.SemaphoreType.DMA((2,)),
             pltpu.SemaphoreType.DMA((3,)),
             pltpu.SemaphoreType.DMA((3,)),
-            pltpu.SemaphoreType.DMA((2,)),
-            pltpu.SemaphoreType.DMA((2,)),
+            pltpu.SemaphoreType.DMA((1,)),
+            pltpu.SemaphoreType.DMA((1,)),
         ],
         compiler_params=pltpu.CompilerParams(
             collective_id=0, has_side_effects=True, vmem_limit_bytes=34 << 20

time: 40.6 us -> 40 us (0.985)
  Pallas kernels: 38.7 us -> 38.1 us
    pallas_call x1, Pallas kernels: 35.7 us -> 35.2 us  [per_device(): pl.pallas_call(powers_kernel, out_shape=[pltpu.VMEM(field, F32)] * 4 + [p...]
where the time goes in v6:
time: 40 us; the launch traced here: 39.9 us
  Pallas kernels  38.1 us (95%)
  between operations  1.51 us (4%)
    pallas_call x1, Pallas kernels, per_device(): pl.pallas_call(powers_kernel, out_shape=[pltpu.VMEM(field, F32)] * 4 + [p...  35.2 us
    pallas_call x1, Pallas kernels, per_device(): pl.pallas_call(combine_kernel, out_shape=[jax.ShapeDtypeStruct(field, F32...  2.94 us

profile of v6, /device:TPU:1, one launch (start us, length us, event | category | flops | bytes accessed | tf_op | source)
XLA Modules:
  0.0 39.9 jit_solution(6965125393887214338)
XLA Ops:
  0.6 0.0 copy-start
  0.6 35.2 %powers.1 = (f32[3,8,64,512]{3,2,1,0:T(8,128)S(1)}, f32[3,8,64,512]{3,2,1,0:T(8,128)S(1)}, f32[3,8,64,512]{3,2,1,0:T(8,128)S(1)}, f32[3,8,64,512]{3,2,1,0:T(8,12...) custom-call(f32[3,8,64,512]{3,2,1,0:T(8,128)} %b_hbm.1, f32[3,8,64,512]{3,2,1,0:T(8,128)} %rad_hbm.1, ...), custom_call_target="tpu_custom_call" | custom-call | tf_op jit(solution)/shard_map/powers/pallas_call | solution.py:702
  36.5 0.0 copy-done
  36.5 2.9 %combine.1 = (f32[3,8,64,512]{3,2,1,0:T(8,128)}, f32[3,8,64,512]{3,2,1,0:T(8,128)}) custom-call(f32[3,6,8,128]{3,2,1,0:T(8,128)S(1)} %get-tuple-element.28.coef, f32[3,8,64,512]{3,2,1,0:T(8,128)S(1)} %get-tuple-element.29.v0, f32[3,8,64,512]{3,2,1,0:T(8,128)S(1)} %get-tuple-element.30.v1, f32[3,8,64,512]{3,2,1,0:T(8,128)S(1)} %get-tuple-element.31.v2, ...), custom_call_target="tpu_custom_call" | custom-call | tf_op jit(solution)/shard_map/combine/pallas_call | solution.py:747
  39.5 0.2 conditional.1
Async XLA Ops:
  0.6 35.9 %copy-start = (f32[3,8,64,512]{3,2,1,0:T(8,128)S(1)}, f32[3,8,64,512]{3,2,1,0:T(8,128)}, u32[]{:S(2)}) copy-start(f32[3,8,64,512]{3,2,1,0:T(8,128)} %b_hbm.1) | copy-start | bytes 9437188

commit v7 on v6

--- a/solution.py
+++ b/solution.py
@@ -645,9 +645,10 @@
 
     others = got.at[pl.ds(0, len(OFFSETS))]
     wait_for(others, sum_recv.at[0])
-    terms = [got[i] for i in range(len(OFFSETS) + 1)]
+    terms = [got[pl.ds(8 * i, 8), 0, :] for i in range((len(OFFSETS) + 1) // 8)]
     while len(terms) > 1:
         terms = [terms[i] + terms[i + 1] for i in range(0, len(terms), 2)]
+    terms = [jnp.sum(terms[0], axis=0, keepdims=True)]
     own = terms[0]
     wait_for(others, sum_send.at[0])
 

time: 40 us -> 40 us (level)
  no operation moved by 1% of the time
where the time goes in v7:
time: 40 us; the launch traced here: 39.9 us
  Pallas kernels  38.1 us (95%)
  between operations  1.51 us (4%)
    pallas_call x1, Pallas kernels, per_device(): pl.pallas_call(powers_kernel, out_shape=[pltpu.VMEM(field, F32)] * 4 + [p...  35.2 us
    pallas_call x1, Pallas kernels, per_device(): pl.pallas_call(combine_kernel, out_shape=[jax.ShapeDtypeStruct(field, F32...  2.94 us

profile of v7, /device:TPU:1, one launch (start us, length us, event | category | flops | bytes accessed | tf_op | source)
XLA Modules:
  0.0 39.9 jit_solution(17914091653585373811)
XLA Ops:
  0.6 0.0 copy-start
  0.6 35.2 %powers.1 = (f32[3,8,64,512]{3,2,1,0:T(8,128)S(1)}, f32[3,8,64,512]{3,2,1,0:T(8,128)S(1)}, f32[3,8,64,512]{3,2,1,0:T(8,128)S(1)}, f32[3,8,64,512]{3,2,1,0:T(8,12...) custom-call(f32[3,8,64,512]{3,2,1,0:T(8,128)} %b_hbm.1, f32[3,8,64,512]{3,2,1,0:T(8,128)} %rad_hbm.1, ...), custom_call_target="tpu_custom_call" | custom-call | tf_op jit(solution)/shard_map/powers/pallas_call | solution.py:703
  36.5 0.0 copy-done
  36.5 2.9 %combine.1 = (f32[3,8,64,512]{3,2,1,0:T(8,128)}, f32[3,8,64,512]{3,2,1,0:T(8,128)}) custom-call(f32[3,6,8,128]{3,2,1,0:T(8,128)S(1)} %get-tuple-element.28.coef, f32[3,8,64,512]{3,2,1,0:T(8,128)S(1)} %get-tuple-element.29.v0, f32[3,8,64,512]{3,2,1,0:T(8,128)S(1)} %get-tuple-element.30.v1, f32[3,8,64,512]{3,2,1,0:T(8,128)S(1)} %get-tuple-element.31.v2, ...), custom_call_target="tpu_custom_call" | custom-call | tf_op jit(solution)/shard_map/combine/pallas_call | solution.py:748
  39.5 0.2 conditional.1
Async XLA Ops:
  0.6 35.9 %copy-start = (f32[3,8,64,512]{3,2,1,0:T(8,128)S(1)}, f32[3,8,64,512]{3,2,1,0:T(8,128)}, u32[]{:S(2)}) copy-start(f32[3,8,64,512]{3,2,1,0:T(8,128)} %b_hbm.1) | copy-start | bytes 9437188
